TPU v7x, 32 devices: a whole 2x2x4 slice. The times are simulated.
32 devices in a mesh: tx: 16 (over z, y, core), ty: 2 (over x).
Axes of the slice: x: 2, y: 2, z: 4, core: 2. Of those that a mesh axis runs over, the one named last changes fastest.
Arguments:
- cells: bfloat16 [16, 2, 512, 512], P('tx', 'ty'), may hold values from -6 to 6
- halo_inputs: bfloat16 [16, 2, 256, 512], P('tx', 'ty'), may hold values from -6 to 6
- stale_halo: bfloat16 [16, 2, 1, 256, 512], P('tx', 'ty'), may hold values from -6 to 6
- stale_returned: bfloat16 [16, 2, 1, 256, 512], P('tx', 'ty'), may hold values from -3 to 3
- cotangent: bfloat16 [16, 2, 512, 512], P('tx', 'ty'), may hold values from -6 to 6
- expression: bfloat16 [16, 2, 512, 512], P('tx', 'ty'), may hold values from -6 to 6
- halo_expression: bfloat16 [16, 2, 256, 512], P('tx', 'ty'), may hold values from -6 to 6
- neighbours: int32 [16, 2, 16, 512], P('tx', 'ty'), may hold values from 0 to 767
- edge_mask: int32 [16, 2, 16, 512], P('tx', 'ty'), may hold values 0 or 1
- send_rows: int32 [16, 2, 8, 32], P('tx', 'ty'), may hold values from 0 to 511
- live_cells: int32 [16, 2], P('tx', 'ty'), may hold values from 256 to 512
- ligand_genes: int32 [1024], replicated, may hold values from 0 to 511
- receptor_genes: int32 [1024], replicated, may hold values from 0 to 511
- gate_weights: float32 [1024], replicated, may hold values from -0.1875 to 0.1875
- self_weights: bfloat16 [2, 512, 512], replicated, may hold values from -0.25 to 0.25
- neighbour_weights: bfloat16 [2, 512, 512], replicated, may hold values from -0.25 to 0.25
Outputs:
- fresh_halo: bfloat16 [16, 2, 1, 256, 512], P('tx', 'ty')
- returned_grads: bfloat16 [16, 2, 1, 256, 512], P('tx', 'ty')
- layer_updates: float32 [4, 512, 512], replicated
- gate_update: float32 [1024], replicated
All inputs are finite; a program needn't handle non-finite values. No bound on the sum of `edge_mask` on one device may be relied on, other than what follows from the above.
Results may differ from a plain program's by a relative error of at most 0.0062.
Values may be sent and summed in bfloat16 or wider, within the bound.
A program may use at most 64 MiB of HBM per device.

v0:
```python
import jax
import jax.numpy as jnp
from jax import lax
from jax.sharding import PartitionSpec as P

OFFSETS = ((-1, -1), (-1, 0), (-1, 1), (0, -1), (0, 1), (1, -1), (1, 0), (1, 1))
HIGHEST = lax.Precision.HIGHEST


def from_behind(value, axis, steps):
    count = lax.axis_size(axis)
    leading, last = (max(0, -steps), min(count, count - steps))
    return lax.ppermute(value, axis, [(source, source + steps) for source in range(leading, last)])


def silu_slope(pre_act):
    sigmoid_value = jax.nn.sigmoid(pre_act)
    return sigmoid_value * (1.0 + pre_act * (1.0 - sigmoid_value))


def along_wide(payload, offset):
    return from_behind(payload, "tx", offset)


def along_narrow(payload, offset):
    return from_behind(payload, "ty", offset)


def route_blocks(blocks, block_axis):
    pieces = {}
    for direction, offset in enumerate(OFFSETS):
        pieces[offset] = lax.index_in_dim(blocks, direction, block_axis, keepdims=False)

    def offset_of(lead_offset, cross_offset):
        return (lead_offset, cross_offset)

    passed = {}
    for lead_offset in (-1, 1):
        payload = jnp.stack(
            [pieces[offset_of(lead_offset, cross_offset)] for cross_offset in (-1, 0, 1)]
        )
        shifted = along_wide(payload, lead_offset)
        for position, cross_offset in enumerate((-1, 0, 1)):
            passed[offset_of(lead_offset, cross_offset)] = shifted[position]
    arrived = {offset_of(-1, 0): passed[offset_of(-1, 0)], offset_of(1, 0): passed[offset_of(1, 0)]}
    for cross_offset in (-1, 1):
        payload = jnp.stack(
            [
                pieces[offset_of(0, cross_offset)],
                passed[offset_of(-1, cross_offset)],
                passed[offset_of(1, cross_offset)],
            ]
        )
        shifted = along_narrow(payload, cross_offset)
        arrived[offset_of(0, cross_offset)] = shifted[0]
        arrived[offset_of(-1, cross_offset)] = shifted[1]
        arrived[offset_of(1, cross_offset)] = shifted[2]
    return jnp.stack([arrived[offset] for offset in OFFSETS], block_axis)


def on_device(
    cells,
    halo_inputs,
    stale_halo,
    stale_returned,
    cotangent,
    expression,
    halo_expression,
    neighbours,
    edge_mask,
    send_rows,
    live_cells,
    ligand_genes,
    receptor_genes,
    gate_weights,
    self_weights,
    neighbour_weights,
):
    own_state = cells[0, 0]
    halo_first = halo_inputs[0, 0]
    stale_rows = stale_halo[0, 0]
    stale_back = stale_returned[0, 0]
    upstream = cotangent[0, 0]
    genes_here = expression[0, 0]
    genes_halo = halo_expression[0, 0]
    neighbour_ids = neighbours[0, 0]
    valid_edges = edge_mask[0, 0]
    outgoing = send_rows[0, 0]
    live_count = live_cells[0, 0]
    layer_total = self_weights.shape[0]
    cell_count, model_width = own_state.shape
    gene_count = genes_here.shape[1]
    joined_count = cell_count + genes_halo.shape[0]
    joined_ids = jnp.arange(joined_count, dtype=jnp.int32)
    edge_table = (neighbour_ids[:, :, None] == joined_ids[None, None, :]).astype(jnp.float32)

    def dense_edges(values):
        return jnp.sum(values[:, :, None] * edge_table, axis=0)

    def pick_edges(matrix):
        return jnp.sum(edge_table * matrix[None], axis=2)

    gene_ids = jnp.arange(gene_count, dtype=jnp.int32)
    ligand_table = (gene_ids[:, None] == ligand_genes[None, :]).astype(jnp.bfloat16)
    receptor_table = (gene_ids[:, None] == receptor_genes[None, :]).astype(jnp.bfloat16)
    all_genes = jnp.concatenate([genes_here, genes_halo], 0)
    ligand = jnp.dot(all_genes, ligand_table, preferred_element_type=jnp.float32).astype(
        jnp.bfloat16
    )
    receptor = jnp.dot(genes_here, receptor_table, preferred_element_type=jnp.float32).astype(
        jnp.bfloat16
    )
    ligand_wide = ligand.astype(jnp.float32)
    scaled = receptor.astype(jnp.float32) * gate_weights[None, :]
    score_table = jnp.dot(scaled, ligand_wide.T, precision=HIGHEST)
    edge_score = pick_edges(score_table)
    gate_value = jax.nn.sigmoid(edge_score)
    weight = 0.25 * valid_edges.astype(jnp.float32) * gate_value
    adjacency = dense_edges(weight)
    cell_ids = jnp.arange(cell_count, dtype=jnp.int32)
    send_table = (outgoing.reshape(-1)[:, None] == cell_ids[None, :]).astype(jnp.bfloat16)
    states = [own_state]
    full_rows = []
    aggregates = []
    pre_acts = []
    for layer_id in range(layer_total):
        halo_rows = halo_first if layer_id == 0 else stale_rows[layer_id - 1]
        joined = jnp.concatenate([states[layer_id], halo_rows], 0)
        aggregate = jnp.dot(adjacency, joined.astype(jnp.float32), precision=HIGHEST).astype(
            jnp.bfloat16
        )
        pre_act = jnp.dot(
            states[layer_id], self_weights[layer_id], preferred_element_type=jnp.float32
        )
        pre_act = pre_act + jnp.dot(
            aggregate, neighbour_weights[layer_id], preferred_element_type=jnp.float32
        )
        full_rows.append(joined)
        aggregates.append(aggregate)
        pre_acts.append(pre_act)
        if layer_id + 1 < layer_total:
            states.append(
                (states[layer_id].astype(jnp.float32) + jax.nn.silu(pre_act)).astype(jnp.bfloat16)
            )
    send_blocks = jnp.stack(
        [
            jnp.dot(send_table, states[1], preferred_element_type=jnp.float32)
            .astype(jnp.bfloat16)
            .reshape(8, -1, model_width)
        ]
    )
    live_rows = (cell_ids < live_count)[:, None]
    grad_state = jnp.where(live_rows, upstream.astype(jnp.float32), jnp.float32(0.0))
    edge_grad = jnp.zeros(neighbour_ids.shape, jnp.float32)
    layer_grads = [None] * (2 * layer_total)
    halo_grads = []
    for layer_id in range(layer_total - 1, -1, -1):
        grad_pre = (grad_state * silu_slope(pre_acts[layer_id])).astype(jnp.bfloat16)
        layer_grads[2 * layer_id] = jnp.dot(
            states[layer_id].T, grad_pre, preferred_element_type=jnp.float32
        )
        layer_grads[2 * layer_id + 1] = jnp.dot(
            aggregates[layer_id].T, grad_pre, preferred_element_type=jnp.float32
        )
        grad_aggregate = jnp.dot(
            grad_pre, neighbour_weights[layer_id].T, preferred_element_type=jnp.float32
        ).astype(jnp.bfloat16)
        joined = full_rows[layer_id]
        inner_table = jnp.dot(grad_aggregate, joined.T, preferred_element_type=jnp.float32)
        edge_grad = edge_grad + pick_edges(inner_table)
        if layer_id > 0:
            grad_full = jnp.dot(adjacency.T, grad_aggregate.astype(jnp.float32), precision=HIGHEST)
            halo_grads.insert(
                0, grad_full[cell_count:].astype(jnp.bfloat16).reshape(8, -1, model_width)
            )
            grad_state = grad_state + jnp.dot(
                grad_pre, self_weights[layer_id].T, preferred_element_type=jnp.float32
            )
            grad_state = grad_state + grad_full[:cell_count]
            grad_state = grad_state + lax.dot_general(
                send_table,
                stale_back[layer_id - 1],
                (((0,), (0,)), ((), ())),
                preferred_element_type=jnp.float32,
            )
    grad_score = (
        0.25 * valid_edges.astype(jnp.float32) * edge_grad * gate_value * (1.0 - gate_value)
    )
    score_grads = dense_edges(grad_score)
    gate_rows = jnp.dot(score_grads, ligand_wide, precision=HIGHEST)
    gate_grad = jnp.sum(gate_rows * receptor.astype(jnp.float32), axis=0)
    backward_blocks = jnp.flip(jnp.stack(halo_grads), 1)
    combined = route_blocks(jnp.stack([send_blocks, backward_blocks]), 2)
    fresh_blocks = combined[0]
    returned_blocks = jnp.flip(combined[1], 1)
    gradient = jnp.concatenate([jnp.stack(layer_grads).reshape(-1), gate_grad])
    summed_all = lax.psum(gradient, ("tx", "ty"))
    square = jnp.sum(summed_all * summed_all)
    clip_factor = jnp.minimum(1.0, 2.0 * model_width / jnp.sqrt(square + 1e-06))
    update = clip_factor * summed_all
    layer_size = 2 * layer_total * model_width * model_width
    layer_part = update[:layer_size].reshape(2 * layer_total, model_width, model_width)
    gate_part = update[layer_size:]
    halo_shape = (1, 1, layer_total - 1, -1, model_width)
    return (
        fresh_blocks.reshape(halo_shape),
        returned_blocks.reshape(halo_shape),
        layer_part,
        gate_part,
    )


def solution(mesh):
    return jax.shard_map(
        on_device,
        mesh=mesh,
        in_specs=(
            P("tx", "ty", None, None),
            P("tx", "ty", None, None),
            P("tx", "ty", None, None, None),
            P("tx", "ty", None, None, None),
            P("tx", "ty", None, None),
            P("tx", "ty", None, None),
            P("tx", "ty", None, None),
            P("tx", "ty", None, None),
            P("tx", "ty", None, None),
            P("tx", "ty", None, None),
            P("tx", "ty"),
            P(),
            P(),
            P(),
            P(),
            P(),
        ),
        out_specs=(P("tx", "ty", None, None, None), P("tx", "ty", None, None, None), P(), P()),
        check_vma=False,
    )
```

profile of v0, /device:TPU:0, one launch (start us, length us, event | category | flops | bytes accessed | tf_op | source)
XLA Modules:
  0.0 251.6 jit_solution(2922967111022507948)
XLA Ops:
  7.3 1.9 fusion.5
  9.2 1.0 fusion.4
  10.3 1.2 copy-done.30
  11.5 2.9 %fusion = f32[512,768]{1,0:T(8,128)S(1)} fusion(bf16[768,1024]{1,0:T(8,128)(2,1)S(1)} %fusion.4, bf16[1024,512]{0,1:T(8,128)(2,1)S(1)} %fusion.5, f32[1024]{0:T(1024)S(1)} %copy-done.29), kind=kOutput, calls=%fused_computation.12 | convolution fusion | flops 4832886784 | bytes 4198400 | tf_op jit(solution)/shard_map/dot_general | solution.py:115
  14.4 4.5 %select_reduce_fusion.4 = f32[16,512]{1,0:T(8,128)S(1)} fusion(f32[512,768]{1,0:T(8,128)S(1)} %fusion, s32[16,512]{1,0:T(8,128)S(1)} %bitcast.169), kind=kLoop, calls=%fused_computation.4 | loop fusion | flops 18866176 | bytes 1638400 | tf_op jit(solution)/shard_map/reduce_sum | solution.py:101
  19.0 3.2 %select_reduce_fusion.3 = f32[512,768]{1,0:T(8,128)S(1)} fusion(f32[16,512]{1,0:T(8,128)S(1)} %bitcast_multiply_fusion.4, s32[16,512]{1,0:T(8,128)S(1)} %bitcast.170), kind=kLoop, calls=%fused_computation.3 | loop fusion | flops 18481152 | bytes 1638400 | tf_op jit(solution)/shard_map/reduce_sum | solution.py:98
  22.7 1.4 convolution_convert_fusion.3
  24.1 1.6 add_convert_fusion
  26.1 0.5 copy-done.15
  26.6 1.4 convolution_convert_fusion.2
  28.7 0.8 fusion.12
  29.5 0.8 copy-done.8
  30.3 0.5 convolution_convert_fusion.1
  30.8 1.5 fusion.77
  32.3 0.8 reverse_bitcast_fusion
  33.6 1.5 fusion.55
  35.1 0.7 pad_maximum_fusion.9
  35.8 3.1 %collective-permute-start.1 = (bf16[3,2,1,32,512]{4,3,1,2,0:T(8,128)(2,1)}, bf16[3,2,1,32,512]{4,3,1,2,0:T(8,128)(2,1)}, u32[]{:S(2)}, u32[]{:S(2)}) collective-permute-start(bf16[3,2,1,32,512]{4,3,1,2,0:T(8,128)(2,1)} %pad_maximum_fusion.9), channel_id=1, source_target_pairs={{0,2},{2,4},{4,6},{6,8},{8,10},{10,12},{12,14},{14,16},{16,18},{18... | collective-permute-start | bytes 589832 | tf_op jit(solution)/shard_map/ppermute | solution.py:13
  38.9 0.7 pad_maximum_fusion.8
  39.6 1.5 collective-permute-start
  41.1 0.6 fusion.31
  41.7 1.5 convolution_bitcast_fusion
  43.2 1.5 convolution_bitcast_fusion.1
  45.4 0.8 fusion.9
  46.2 3.3 %fusion.10 = f32[512,768]{1,0:T(8,128)} fusion(bf16[512,512]{1,0:T(8,128)(2,1)S(1)} %fusion.9, bf16[256,512]{1,0:T(8,128)(2,1)} %bitcast.176, bf16[512,512]{1,0:T(8,128)(2,1)S(1)} %bitcast.165, bf16[2,512,512]{2,1,0:T(8,128)(2,1)} %param.31), kind=kOutput, calls=%fused_computation.35 | convolution fusion | flops 672923648 | bytes 3407872 | tf_op jit(solution)/shard_map/dot_general | solution.py:169
  49.5 0.5 convolution_bitcast_fusion.2
  50.9 9.0 %select_reduce_fusion.1 = (f32[16,512]{1,0:T(8,128)S(1)}, f32[16,512]{1,0:T(8,128)S(1)}) fusion(f32[512,768]{1,0:T(8,128)S(1)} %copy-done.12, s32[16,512]{1,0:T(8,128)S(1)} %bitcast.171, f32[512,768]{1,0:T(8,128)S(1)} %fusion.31), kind=kLoop, calls=%fused_computation.1 | loop fusion | flops 31440896 | bytes 3244032 | tf_op jit(solution)/shard_map/reduce_sum | solution.py:101
  60.0 3.2 %select_reduce_fusion = f32[512,768]{1,0:T(8,128)S(1)} fusion(f32[16,512]{1,0:T(8,128)S(1)} %fusion.66, s32[16,512]{1,0:T(8,128)S(1)} %bitcast.172), kind=kLoop, calls=%fused_computation | loop fusion | flops 18481152 | bytes 1638400 | tf_op jit(solution)/shard_map/reduce_sum | solution.py:98
  63.2 2.5 pad_maximum_fusion.1
  65.6 5.2 %copy.51 = f32[4,512,512]{2,1,0:T(8,128)} copy(f32[4,512,512]{1,2,0:T(8,128)} %pad_maximum_fusion.1) | data formatting | bytes 8388608 | tf_op jit(solution)/shard_map/stack | solution.py:196
  70.9 3.4 %copy.62 = f32[256,4,8,128]{3,1,2,0:T(4,128)S(1)} copy(f32[256,4,8,128]{3,2,1,0:T(8,128)} %bitcast.163) | data formatting | bytes 8388608
  74.3 2.7 %fusion.1 = f32[1024]{0:T(1024)S(1)} fusion(bf16[1024,512]{0,1:T(8,128)(2,1)S(1)} %copy-done.33, f32[512,768]{1,0:T(8,128)S(1)} %select_reduce_fusion, bf16[768,1024]{1,0:T(8,128)(2,1)S(1)} %copy-done.31), kind=kOutput, calls=%fused_computation.13 | convolution fusion | flops 4833410048 | bytes 4198400 | tf_op jit(solution)/shard_map/dot_general | solution.py:190
  77.0 0.9 fusion.76
  77.9 0.9 fusion.75
  78.8 1.3 collective-permute-start.2
  80.1 2.6 %pad_maximum_fusion = f32[1049600]{0:T(1024)} fusion(f32[1024]{0:T(1024)S(1)} %fusion.1, f32[1048576]{0:T(1024)S(1)} %bitcast.162), kind=kLoop, calls=%fused_computation.6 | loop fusion | flops 1049600 | bytes 8396800 | tf_op jit(solution)/shard_map/concatenate | solution.py:196
  82.8 4.6 %collective-permute-start.3 = (bf16[3,2,1,32,512]{4,3,1,2,0:T(8,128)(2,1)S(1)}, bf16[3,2,1,32,512]{4,3,1,2,0:T(8,128)(2,1)S(1)}, u32[]{:S(2)}, u32[]{:S(2)}) collective-permute-start(bf16[3,2,1,32,512]{4,3,1,2,0:T(8,128)(2,1)S(1)} %pad_maximum_fusion.11), channel_id=1, source_target_pairs={{0,1},{2,3},{4,5},{6,7},{8,9},{10,11},{12,13},{14,15},{16,17},{18,... | collective-permute-start | bytes 589832 | tf_op jit(solution)/shard_map/ppermute | solution.py:13
  87.4 0.8 fusion.56
  88.2 3.0 %collective-permute-done.3 = bf16[3,2,1,32,512]{4,3,1,2,0:T(8,128)(2,1)S(1)} collective-permute-done((bf16[3,2,1,32,512]{4,3,1,2,0:T(8,128)(2,1)S(1)}, bf16[3,2,1,32,512]{4,3,1,2,0:T(8,128)(2,1)S(1)}, u32[]{:S(2)}, u32[]{:S(2)}) %collective-permute-start.3) | collective-permute-done | bytes 196640 | tf_op jit(solution)/shard_map/ppermute | solution.py:13
  91.3 0.8 fusion.50
  92.2 0.7 slice_bitcast_fusion
  92.9 0.7 rev.8
  93.6 137.0 %all-reduce.2.cloned.1.call-done = f32[1049600]{0:T(1024)} async-done(((f32[1049600]{0:T(1024)}), f32[1049600]{0:T(1024)}) %all-reduce.2.cloned.1.call-update) | async-done | bytes 4198416 | tf_op jit(solution)/shard_map/psum | solution.py:197
  230.6 3.4 %multiply_reduce_fusion = f32[]{:T(128)} fusion(f32[1049600]{0:T(1024)} %all-reduce.2.cloned.1.call-done), kind=kLoop, calls=%fused_computation.7 | loop fusion | flops 2099199 | bytes 4198404 | tf_op jit(solution)/shard_map/reduce_sum | solution.py:198
  234.7 2.4 broadcast_multiply_fusion
  237.1 2.2 slice.154
  239.3 0.6 slice.155
  239.9 4.9 %reshape.63 = f32[4,512,512]{2,1,0:T(8,128)} reshape(f32[1048576]{0:T(1024)} %slice.154) | data formatting | bytes 8388608 | tf_op jit(solution)/shard_map/reshape | solution.py:202
  (90 shorter events, 3.3 us)
Async XLA Ops:
  7.2 37.5 %copy-start = (bf16[1,1,1,256,512]{4,3,2,1,0:T(8,128)(2,1)S(1)}, bf16[1,1,1,256,512]{4,3,2,1,0:T(8,128)(2,1)}, u32[]{:S(2)}) copy-start(bf16[1,1,1,256,512]{4,3,2,1,0:T(8,128)(2,1)} %param.19) | copy-start | bytes 786436
  7.2 2.0 copy-start.24
  7.2 2.0 copy-start.28
  7.2 2.0 copy-start.27
  7.2 223.4 %all-reduce.2.cloned.1.call-start = ((), (), s32[]{:S(2)}) async-start(), calls=%async_computation | async-start | bytes 8396800 | tf_op jit(solution)/shard_map/psum | solution.py:197
  9.2 1.1 copy-start.32
  9.2 2.2 copy-start.29
  10.3 1.2 copy-start.30
  11.5 2.9 %copy-start.17 = (s32[1,1,16,512]{3,2,1,0:T(8,128)S(1)}, s32[1,1,16,512]{3,2,1,0:T(8,128)}, u32[]{:S(2)}) copy-start(s32[1,1,16,512]{3,2,1,0:T(8,128)} %param.23) | copy-start | bytes 98308
  11.5 7.5 %copy-start.20 = (s32[1,1,16,512]{3,2,1,0:T(8,128)S(1)}, s32[1,1,16,512]{3,2,1,0:T(8,128)}, u32[]{:S(2)}) copy-start(s32[1,1,16,512]{3,2,1,0:T(8,128)} %param.24) | copy-start | bytes 98308
  14.3 7.8 %copy-start.1 = (bf16[1,1,512,512]{3,2,1,0:T(8,128)(2,1)S(1)}, bf16[1,1,512,512]{3,2,1,0:T(8,128)(2,1)}, u32[]{:S(2)}) copy-start(bf16[1,1,512,512]{3,2,1,0:T(8,128)(2,1)} %param.16) | copy-start | bytes 1572868
  14.4 7.8 %copy-start.13 = (bf16[2,512,512]{2,1,0:T(8,128)(2,1)S(1)}, bf16[2,512,512]{2,1,0:T(8,128)(2,1)}, u32[]{:S(2)}) copy-start(bf16[2,512,512]{2,1,0:T(8,128)(2,1)} %param.30) | copy-start | bytes 3145732
  18.9 3.7 %copy-start.19 = (bf16[1,1,256,512]{3,2,1,0:T(8,128)(2,1)S(1)}, bf16[1,1,256,512]{3,2,1,0:T(8,128)(2,1)}, u32[]{:S(2)}) copy-start(bf16[1,1,256,512]{3,2,1,0:T(8,128)(2,1)} %param.17) | copy-start | bytes 786436
  22.2 1.9 copy-start.23
  24.1 1.6 copy-start.6
  25.7 1.0 copy-start.15
  25.7 3.0 %copy-start.25 = (bf16[1,1,512,512]{3,2,1,0:T(8,128)(2,1)S(1)}, bf16[1,1,512,512]{3,2,1,0:T(8,128)(2,1)}, u32[]{:S(2)}) copy-start(bf16[1,1,512,512]{3,2,1,0:T(8,128)(2,1)} %param.20) | copy-start | bytes 1572868
  28.1 1.4 copy-start.10
  29.5 0.8 copy-start.8
  30.8 2.4 copy-start.22
  32.3 7.3 %copy-start.4 = (f32[768,512]{1,0:T(8,128)}, f32[768,512]{1,0:T(8,128)S(1)}, u32[]{:S(2)}) copy-start(f32[768,512]{1,0:T(8,128)S(1)} %fusion.77) | copy-start | bytes 4718596
  33.2 7.8 %copy-start.16 = (bf16[1,1,1,256,512]{4,3,2,1,0:T(8,128)(2,1)S(1)}, bf16[1,1,1,256,512]{4,3,2,1,0:T(8,128)(2,1)}, u32[]{:S(2)}) copy-start(bf16[1,1,1,256,512]{4,3,2,1,0:T(8,128)(2,1)} %param.18) | copy-start | bytes 786436
  35.1 6.6 %copy-start.9 = (bf16[512,512]{1,0:T(8,128)(2,1)S(1)}, bf16[512,512]{1,0:T(8,128)(2,1)}, u32[]{:S(2)}) copy-start(bf16[512,512]{1,0:T(8,128)(2,1)} %copy-done.8) | copy-start | bytes 1572868
  35.1 6.6 %copy-start.11 = (bf16[512,512]{1,0:T(8,128)(2,1)S(1)}, bf16[512,512]{1,0:T(8,128)(2,1)}, u32[]{:S(2)}) copy-start(bf16[512,512]{1,0:T(8,128)(2,1)} %copy-done.10) | copy-start | bytes 1572868
  35.8 41.2 %collective-permute-start.1 = (bf16[3,2,1,32,512]{4,3,1,2,0:T(8,128)(2,1)}, bf16[3,2,1,32,512]{4,3,1,2,0:T(8,128)(2,1)}, u32[]{:S(2)}, u32[]{:S(2)}) collective-permute-start(bf16[3,2,1,32,512]{4,3,1,2,0:T(8,128)(2,1)} %pad_maximum_fusion.9), channel_id=1, source_target_pairs={{0,2},{2,4},{4,6},{6,8},{8,10},{10,12},{12,14},{14,16},{16,18},{18... | collective-permute-start | bytes 589832 | tf_op jit(solution)/shard_map/ppermute | solution.py:13
  39.6 38.3 %collective-permute-start = (bf16[3,2,1,32,512]{4,3,1,2,0:T(8,128)(2,1)}, bf16[3,2,1,32,512]{4,3,1,2,0:T(8,128)(2,1)}, u32[]{:S(2)}, u32[]{:S(2)}) collective-permute-start(bf16[3,2,1,32,512]{4,3,1,2,0:T(8,128)(2,1)} %pad_maximum_fusion.8), channel_id=1, source_target_pairs={{2,0},{4,2},{6,4},{8,6},{10,8},{12,10},{14,12},{16,14},{18,16},{20... | collective-permute-start | bytes 589832 | tf_op jit(solution)/shard_map/ppermute | solution.py:13
  41.7 3.4 %copy-start.34 = (f32[512,512]{1,0:T(8,128)S(1)}, f32[512,512]{1,0:T(8,128)}, u32[]{:S(2)}) copy-start(f32[512,512]{1,0:T(8,128)} %get-tuple-element.21) | copy-start | bytes 3145732
  43.2 1.9 copy-start.5
  43.2 2.1 copy-start.14
  43.2 2.2 copy-start.26
  46.2 3.3 %copy-start.7 = (bf16[512,512]{1,0:T(8,128)(2,1)S(1)}, bf16[512,512]{1,0:T(8,128)(2,1)}, u32[]{:S(2)}) copy-start(bf16[512,512]{1,0:T(8,128)(2,1)} %copy-done.6) | copy-start | bytes 1572868
  49.5 1.4 copy-start.12
  50.9 9.0 %copy-start.21 = (s32[1,1,16,512]{3,2,1,0:T(8,128)S(1)}, s32[1,1,16,512]{3,2,1,0:T(8,128)}, u32[]{:S(2)}) copy-start(s32[1,1,16,512]{3,2,1,0:T(8,128)} %param.24) | copy-start | bytes 98308
  50.9 12.2 %copy-start.2 = (f32[1,512,512]{1,2,0:T(8,128)S(1)}, f32[1,512,512]{1,2,0:T(8,128)}, u32[]{:S(2)}) copy-start(f32[1,512,512]{1,2,0:T(8,128)} %convolution_bitcast_fusion) | copy-start | bytes 3145732
  50.9 12.2 %copy-start.3 = (f32[1,512,512]{1,2,0:T(8,128)S(1)}, f32[1,512,512]{1,2,0:T(8,128)}, u32[]{:S(2)}) copy-start(f32[1,512,512]{1,2,0:T(8,128)} %convolution_bitcast_fusion.1) | copy-start | bytes 3145732
  70.8 3.4 %copy-start.31 = (bf16[768,1024]{1,0:T(8,128)(2,1)S(1)}, bf16[768,1024]{1,0:T(8,128)(2,1)}, u32[]{:S(2)}) copy-start(bf16[768,1024]{1,0:T(8,128)(2,1)} %copy-done.30) | copy-start | bytes 4718596
  70.9 3.4 %copy-start.33 = (bf16[1024,512]{0,1:T(8,128)(2,1)S(1)}, bf16[1024,512]{0,1:T(8,128)(2,1)}, u32[]{:S(2)}) copy-start(bf16[1024,512]{0,1:T(8,128)(2,1)} %copy-done.32) | copy-start | bytes 3145732
  74.3 4.5 %copy-start.18 = (bf16[1,2,1,32,512]{4,3,1,2,0:T(8,128)(2,1)S(1)}, bf16[1,2,1,32,512]{4,3,1,2,0:T(8,128)(2,1)}, u32[]{:S(2)}) copy-start(bf16[1,2,1,32,512]{4,3,1,2,0:T(8,128)(2,1)} %get-tuple-element.9) | copy-start | bytes 196612
  78.8 8.5 %collective-permute-start.2 = (bf16[3,2,1,32,512]{4,3,1,2,0:T(8,128)(2,1)S(1)}, bf16[3,2,1,32,512]{4,3,1,2,0:T(8,128)(2,1)S(1)}, u32[]{:S(2)}, u32[]{:S(2)}) collective-permute-start(bf16[3,2,1,32,512]{4,3,1,2,0:T(8,128)(2,1)S(1)} %pad_maximum_fusion.10), channel_id=1, source_target_pairs={{1,0},{3,2},{5,4},{7,6},{9,8},{11,10},{13,12},{15,14},{17,16},{19,... | collective-permute-start | bytes 589832 | tf_op jit(solution)/shard_map/ppermute | solution.py:13
  82.8 8.5 %collective-permute-start.3 = (bf16[3,2,1,32,512]{4,3,1,2,0:T(8,128)(2,1)S(1)}, bf16[3,2,1,32,512]{4,3,1,2,0:T(8,128)(2,1)S(1)}, u32[]{:S(2)}, u32[]{:S(2)}) collective-permute-start(bf16[3,2,1,32,512]{4,3,1,2,0:T(8,128)(2,1)S(1)} %pad_maximum_fusion.11), channel_id=1, source_target_pairs={{0,1},{2,3},{4,5},{6,7},{8,9},{10,11},{12,13},{14,15},{16,17},{18,... | collective-permute-start | bytes 589832 | tf_op jit(solution)/shard_map/ppermute | solution.py:13
Sparse Core Ops, SparseCore 0:
  82.9 147.6 all-reduce.1
where the time goes:
time: 252 us
  waiting for transfers between devices  140 us (56%)
  other arithmetic  33.7 us (13%)
  matrix products  25.9 us (10%)
  local copies, waits for them, and re-layouts  25.6 us (10%)
  between operations  16 us (6%)
  starting transfers between devices  10.4 us (4%)
    psum x1, waiting for transfers between devices, on_device(): summed_all = lax.psum(gradient, ('tx', 'ty'))  137 us
    reduce_sum x2, other arithmetic, pick_edges(): return jnp.sum(edge_table * matrix[None], axis=2)  13.5 us
    ppermute x4, starting transfers between devices, from_behind(): lax.ppermute(value, axis, [(source, source + steps) for source in range(l...  10.4 us
    unnamed x78, local copies, waits for them, and re-layouts  8.46 us
    reduce_sum x2, other arithmetic, dense_edges(): return jnp.sum(values[:, :, None] * edge_table, axis=0)  6.36 us
    another operation x1, local copies, waits for them, and re-layouts, on_device(): gradient = jnp.concatenate([jnp.stack(layer_grads).reshape(-1), gate_grad])  5.23 us
  transfers between devices with their start and end apart: 5, of which 2 were waited for; matrix products, arithmetic and copies ran while one was open for 17% of the time, Pallas kernels for 0%

commit v1 on v0

v1 whole, which is shorter than its diff:
```python
import functools

import jax
import jax.numpy as jnp
from jax import lax
from jax.experimental import pallas as pl
from jax.experimental.pallas import tpu as pltpu
from jax.sharding import PartitionSpec as P

OFFSETS = ((-1, -1), (-1, 0), (-1, 1), (0, -1), (0, 1), (1, -1), (1, 0), (1, 1))
F32 = jnp.float32
BF16 = jnp.bfloat16


def mm(a, b):
    return jnp.dot(a, b, preferred_element_type=F32)


def mm_nt(a, b):
    return lax.dot_general(a, b, (((1,), (1,)), ((), ())), preferred_element_type=F32)


def mm_tn(a, b):
    return lax.dot_general(a, b, (((0,), (0,)), ((), ())), preferred_element_type=F32)


def split(value):
    high = value.astype(BF16)
    return high, (value - high.astype(F32)).astype(BF16)


def sigmoid(value):
    return jax.nn.sigmoid(value)


def silu_slope(pre_act):
    gate = sigmoid(pre_act)
    return gate * (1.0 + pre_act * (1.0 - gate))


def count_edges(nbr_ref, mask_ref, count_ref):
    degree, cells = nbr_ref.shape[2:]
    rows = count_ref.shape[0]
    step = 32
    for lane in range(0, cells, 128):
        ids = []
        for k in range(degree):
            here = nbr_ref[0, 0, k : k + 1, lane : lane + 128]
            real = mask_ref[0, 0, k : k + 1, lane : lane + 128]
            ids.append(jnp.broadcast_to(jnp.where(real > 0, here, -1), (8, 128)))

        def body(chunk, carry):
            base = chunk * step
            for part in range(0, step, 8):
                row = lax.broadcasted_iota(jnp.int32, (8, 128), 0) + (base + part)
                total = jnp.zeros((8, 128), F32)
                for k in range(degree):
                    total = total + jnp.where(ids[k] == row, 1.0, 0.0)
                count_ref[pl.ds(pl.multiple_of(base + part, 8), 8), lane : lane + 128] = total
            return carry

        lax.fori_loop(0, rows // step, body, 0)


def one_hot(ids, rows):
    return lax.broadcasted_iota(jnp.int32, (rows, ids.shape[1]), 0) == ids


def flat_rows(send_ref):
    directions, border = send_ref.shape[2:]
    total = directions * border
    ids = send_ref[0, 0]
    spread = (
        lax.broadcasted_iota(jnp.int32, (border, total), 1) % border
        == lax.broadcasted_iota(jnp.int32, (border, total), 0)
    ).astype(BF16)
    high = mm((ids // 256).astype(F32).astype(BF16), spread)
    low = mm((ids % 256).astype(F32).astype(BF16), spread)
    wide = high * 256.0 + low
    mine = lax.broadcasted_iota(
        jnp.int32, (directions, total), 1
    ) // border == lax.broadcasted_iota(jnp.int32, (directions, total), 0)
    return jnp.sum(jnp.where(mine, wide, 0.0), axis=0, keepdims=True).astype(jnp.int32)


def tile_kernel(
    live_ref,
    cells_ref,
    halo_ref,
    stale_halo_ref,
    stale_ret_ref,
    cot_ref,
    expr_ref,
    halo_expr_ref,
    nbr_ref,
    mask_ref,
    send_ref,
    lig_ref,
    rec_ref,
    gate_ref,
    self_ref,
    neigh_ref,
    sent_ref,
    halo_grad_ref,
    grads_ref,
    gate_grad_ref,
    count_ref,
    adj_t_ref,
    adj_low_ref,
    slope_ref,
    prod_ref,
    genes_ref,
):
    layers = self_ref.shape[0]
    cells, width = cells_ref.shape[2:]
    halo = halo_ref.shape[2]
    joined_rows = cells + halo
    genes = expr_ref.shape[3]
    chunk = halo

    count_edges(nbr_ref, mask_ref, count_ref)

    receptor_hot = one_hot(rec_ref[...], genes)
    ligand_hot = one_hot(lig_ref[...], genes).astype(BF16)
    gate_high, gate_low = split(gate_ref[...])
    zero = jnp.zeros((), BF16)
    mix = mm_nt(jnp.where(receptor_hot, gate_high, zero), ligand_hot)
    mix = mix + mm_nt(jnp.where(receptor_hot, gate_low, zero), ligand_hot)
    mix_high, mix_low = split(mix)
    expr = expr_ref[0, 0]
    scaled_high, scaled_low = split(mm(expr, mix_high) + mm(expr, mix_low))
    genes_ref[0:cells, :] = expr
    genes_ref[cells:, :] = halo_expr_ref[0, 0]

    def score_chunk(step, carry):
        rows = pl.ds(pl.multiple_of(step * chunk, chunk), chunk)
        here = genes_ref[rows, :]
        score = mm_nt(here, scaled_high) + mm_nt(here, scaled_low)
        gate = sigmoid(score)
        base = 0.25 * count_ref[rows, :] * gate
        high, low = split(base)
        adj_t_ref[rows, :] = high
        adj_low_ref[rows, :] = low
        slope_ref[rows, :] = base * (1.0 - gate)
        return carry

    lax.fori_loop(0, joined_rows // chunk, score_chunk, 0)

    adjacency = adj_t_ref[...].T
    adjacency_low = adj_low_ref[...].T
    state = cells_ref[0, 0]
    states, full_rows, aggregates, pre_acts = [], [], [], []
    for layer in range(layers):
        halo_rows = halo_ref[0, 0] if layer == 0 else stale_halo_ref[0, 0, layer - 1]
        joined = jnp.concatenate([state, halo_rows], 0)
        aggregate = (mm(adjacency, joined) + mm(adjacency_low, joined)).astype(BF16)
        pre_act = mm(state, self_ref[layer]) + mm(aggregate, neigh_ref[layer])
        states.append(state)
        full_rows.append(joined)
        aggregates.append(aggregate)
        pre_acts.append(pre_act)
        if layer + 1 < layers:
            state = (state.astype(F32) + pre_act * sigmoid(pre_act)).astype(BF16)

    send_table = one_hot(flat_rows(send_ref), cells).astype(BF16)
    for layer in range(1, layers):
        sent_ref[layer - 1] = mm_tn(send_table, states[layer]).astype(BF16)

    live = lax.broadcasted_iota(jnp.int32, (cells, width), 0) < live_ref[0, 0]
    grad_state = jnp.where(live, cot_ref[0, 0].astype(F32), 0.0)
    grad_aggregates = [None] * layers
    for layer in range(layers - 1, -1, -1):
        grad_pre = (grad_state * silu_slope(pre_acts[layer])).astype(BF16)
        grads_ref[2 * layer] = mm_tn(states[layer], grad_pre)
        grads_ref[2 * layer + 1] = mm_tn(aggregates[layer], grad_pre)
        grad_aggregate = mm_nt(grad_pre, neigh_ref[layer]).astype(BF16)
        grad_aggregates[layer] = grad_aggregate
        if layer > 0:
            grad_full = mm(adj_t_ref[...], grad_aggregate)
            halo_grad_ref[layer - 1] = grad_full[cells:].astype(BF16)
            grad_state = (
                grad_state
                + mm_nt(grad_pre, self_ref[layer])
                + grad_full[:cells]
                + mm(send_table, stale_ret_ref[0, 0, layer - 1])
            )

    for start in range(0, joined_rows, chunk):
        inner = jnp.zeros((chunk, cells), F32)
        for layer in range(layers):
            inner = inner + mm_nt(
                full_rows[layer][start : start + chunk], grad_aggregates[layer]
            )
        score_grad = (slope_ref[start : start + chunk, :] * inner).astype(BF16)
        prod_ref[start : start + chunk, :] = mm(score_grad, expr).astype(BF16)
    pair_grads = mm_tn(genes_ref[...], prod_ref[...]).astype(BF16)
    picked = mm(pair_grads, receptor_hot.astype(BF16))
    gate_grad_ref[...] = jnp.sum(picked * ligand_hot.astype(F32), axis=0, keepdims=True)


def run_tile(*args):
    (
        cells,
        halo_inputs,
        stale_halo,
        stale_returned,
        cotangent,
        expression,
        halo_expression,
        neighbours,
        edge_mask,
        send_rows,
        live_cells,
        ligand_genes,
        receptor_genes,
        gate_weights,
        self_weights,
        neighbour_weights,
    ) = args
    layers, width, _ = self_weights.shape
    count, halo = cells.shape[2], halo_inputs.shape[2]
    genes, pairs = expression.shape[3], ligand_genes.shape[0]
    vmem = pl.BlockSpec(memory_space=pltpu.VMEM)
    smem = pl.BlockSpec(memory_space=pltpu.SMEM)
    return pl.pallas_call(
        tile_kernel,
        out_shape=(
            jax.ShapeDtypeStruct((layers - 1, halo, width), BF16),
            jax.ShapeDtypeStruct((layers - 1, halo, width), BF16),
            jax.ShapeDtypeStruct((2 * layers, width, width), F32),
            jax.ShapeDtypeStruct((1, pairs), F32),
        ),
        in_specs=[smem] + [vmem] * 15,
        out_specs=(vmem,) * 4,
        scratch_shapes=[
            pltpu.VMEM((count + halo, count), F32),
            pltpu.VMEM((count + halo, count), BF16),
            pltpu.VMEM((count + halo, count), BF16),
            pltpu.VMEM((count + halo, count), F32),
            pltpu.VMEM((count + halo, genes), BF16),
            pltpu.VMEM((count + halo, genes), BF16),
        ],
        compiler_params=pltpu.CompilerParams(vmem_limit_bytes=48 * 1024 * 1024),
        name="tile",
    )(
        live_cells,
        cells,
        halo_inputs,
        stale_halo,
        stale_returned,
        cotangent,
        expression,
        halo_expression,
        neighbours,
        edge_mask,
        send_rows,
        ligand_genes.reshape(1, -1),
        receptor_genes.reshape(1, -1),
        gate_weights.reshape(1, -1),
        self_weights,
        neighbour_weights,
    )


def shift(value, axis, steps):
    count = lax.axis_size(axis)
    first, last = max(0, -steps), min(count, count - steps)
    return lax.ppermute(value, axis, [(source, source + steps) for source in range(first, last)])


def route_blocks(blocks, block_axis):
    pieces = {}
    for direction, offset in enumerate(OFFSETS):
        pieces[offset] = lax.index_in_dim(blocks, direction, block_axis, keepdims=False)
    passed = {}
    for lead in (-1, 1):
        moved = shift(jnp.stack([pieces[lead, cross] for cross in (-1, 0, 1)]), "tx", lead)
        for position, cross in enumerate((-1, 0, 1)):
            passed[lead, cross] = moved[position]
    arrived = {(-1, 0): passed[-1, 0], (1, 0): passed[1, 0]}
    for cross in (-1, 1):
        payload = jnp.stack([pieces[0, cross], passed[-1, cross], passed[1, cross]])
        moved = shift(payload, "ty", cross)
        arrived[0, cross] = moved[0]
        arrived[-1, cross] = moved[1]
        arrived[1, cross] = moved[2]
    return jnp.stack([arrived[offset] for offset in OFFSETS], block_axis)


def on_device(*args):
    self_weights = args[14]
    layers, width, _ = self_weights.shape
    sent, halo_grads, layer_grads, gate_grad = run_tile(*args)
    sent_blocks = sent.reshape(layers - 1, 8, -1, width)
    grad_blocks = jnp.flip(halo_grads.reshape(layers - 1, 8, -1, width), 1)
    combined = route_blocks(jnp.stack([sent_blocks, grad_blocks]), 2)
    returned = jnp.flip(combined[1], 1)
    layer_sum, gate_sum = lax.psum((layer_grads, gate_grad[0]), ("tx", "ty"))
    square = jnp.sum(layer_sum * layer_sum) + jnp.sum(gate_sum * gate_sum)
    clip = jnp.minimum(1.0, 2.0 * width / jnp.sqrt(square + 1e-06))
    halo_shape = (1, 1, layers - 1, -1, width)
    return (
        combined[0].reshape(halo_shape),
        returned.reshape(halo_shape),
        clip * layer_sum,
        clip * gate_sum,
    )


def solution(mesh):
    tile = P("tx", "ty")
    return jax.shard_map(
        on_device,
        mesh=mesh,
        in_specs=(tile,) * 11 + (P(),) * 5,
        out_specs=(tile, tile, P(), P()),
        check_vma=False,
    )
```

time: 252 us -> 205 us (0.81)
  waiting for transfers between devices: 140 us -> 92.3 us
  blocking collectives: 0 us -> 44.2 us
  matrix products: 25.9 us -> 0 us
  other arithmetic: 33.7 us -> 9.91 us
  Pallas kernels: 0 us -> 16.7 us
  local copies, waits for them, and re-layouts: 25.6 us -> 15.2 us
    psum x1, waiting for transfers between devices: 137 us -> 89.1 us  [on_device(): layer_sum, gate_sum = lax.psum((layer_grads, gate_grad[0]), ('tx', 'ty'))]
    psum x0 -> x1, blocking collectives: none -> 44.2 us  [on_device(): layer_sum, gate_sum = lax.psum((layer_grads, gate_grad[0]), ('tx', 'ty'))]
    dot_general x21 -> x0, matrix products: 25.9 us -> none  [the longest x2 3.93 us: on_device(): jnp.dot(grad_aggregate, joined.T, preferred_element_type=jnp.float32)]
    reduce_sum x5 -> x2, other arithmetic: 23.2 us -> 4.47 us  [on_device(): square = jnp.sum(layer_sum * layer_sum) + jnp.sum(gate_sum * gate_sum)]
    pallas_call x0 -> x1, Pallas kernels: none -> 16.7 us  [run_tile(): pl.pallas_call(tile_kernel, out_shape=(jax.ShapeDtypeStruct((layers - 1,...]
    another operation x2 -> x1, local copies, waits for them, and re-layouts: 6.06 us -> 0.02 us  [on_device(): combined = route_blocks(jnp.stack([sent_blocks, grad_blocks]), 2)]
    another operation x6 -> x5, other arithmetic: 5.46 us -> 0.15 us  [the longest x3 0.1 us: route_blocks(): payload = jnp.stack([pieces[0, cross], passed[-1, cross], passed[1, cross]])]
    unnamed x78 -> x37, local copies, waits for them, and re-layouts: 8.46 us -> 13.7 us
  transfers between devices with their start and end apart: 5 -> 5, of which waited for: 2 -> 3; matrix products, arithmetic and copies ran while one was open for 17% -> 1% of each run, Pallas kernels for 0% -> 0%
where the time goes in v1:
time: 205 us; the launch traced here: 204 us
  waiting for transfers between devices  92.3 us (45%)
  blocking collectives  44.2 us (22%)
  Pallas kernels  16.7 us (8%)
  between operations  16.1 us (8%)
  local copies, waits for them, and re-layouts  15.2 us (7%)
  other arithmetic  9.91 us (5%)
  starting transfers between devices  9.58 us (5%)
    psum x1, waiting for transfers between devices, on_device(): layer_sum, gate_sum = lax.psum((layer_grads, gate_grad[0]), ('tx', 'ty'))  89.1 us
    psum x1, blocking collectives, on_device(): layer_sum, gate_sum = lax.psum((layer_grads, gate_grad[0]), ('tx', 'ty'))  44.2 us
    pallas_call x1, Pallas kernels, run_tile(): pl.pallas_call(tile_kernel, out_shape=(jax.ShapeDtypeStruct((layers - 1,...  16.7 us
    unnamed x37, local copies, waits for them, and re-layouts  13.7 us
    ppermute x4, starting transfers between devices, shift(): lax.ppermute(value, axis, [(source, source + steps) for source in range(f...  9.54 us
    mul x1, other arithmetic, on_device(): clip * layer_sum  4.69 us
    reduce_sum x2, other arithmetic, on_device(): square = jnp.sum(layer_sum * layer_sum) + jnp.sum(gate_sum * gate_sum)  4.47 us
  transfers between devices with their start and end apart: 5, of which 3 were waited for; matrix products, arithmetic and copies ran while one was open for 1% of the time, Pallas kernels for 0%

profile of v1, /device:TPU:0, one launch (start us, length us, event | category | flops | bytes accessed | tf_op | source)
XLA Modules:
  0.0 203.9 jit_solution(15622541560972737158)
XLA Ops:
  7.2 0.0 all-reduce.2.cloned.1.call-start
  7.9 0.0 copy-start
  7.9 1.2 copy-done
  9.1 0.0 copy-start.1
  9.1 1.2 copy-done.1
  10.3 0.0 copy-start.2
  10.3 1.0 copy-done.2
  11.4 0.0 copy-start.3
  11.4 1.0 copy-done.3
  12.4 0.0 copy-start.4
  12.4 1.0 copy-done.4
  13.4 0.0 copy-start.5
  13.4 0.9 copy-done.5
  14.4 0.0 copy-start.6
  14.4 0.9 copy-done.6
  15.3 0.0 copy-start.7
  15.3 0.9 copy-done.7
  16.3 0.0 copy-start.8
  16.3 0.9 copy-done.8
  17.2 0.0 copy-start.9
  17.2 0.8 copy-done.9
  18.0 0.8 copy-done.10
  18.8 0.0 copy-start.11
  18.8 0.7 copy-done.11
  19.4 0.0 copy-start.12
  19.4 0.7 copy-done.12
  20.1 0.0 copy-start.13
  20.1 0.7 copy-done.13
  20.8 0.0 copy-start.14
  20.8 0.7 copy-done.14
  21.5 16.7 %tile.1 = (bf16[1,256,512]{2,1,0:T(8,128)(2,1)S(1)}, bf16[1,256,512]{2,1,0:T(8,128)(2,1)S(1)}, f32[4,512,512]{2,1,0:T(8,128)}, f32[1,1024]{1,0:T(1,128)S(1)}) custom-call(s32[1,1]{1,0:T(1,128)S(6)} %copy.42.live_ref, bf16[1,1,512,512]{3,2,1,0:T(8,128)(2,1)S(1)} %copy-done.2, bf16[1,1,256,512]{3,2,1,0:T(8,128)(2,1)S(1)} %copy-done.5, ...), custom_call_target="tpu_custom_call" | custom-call | tf_op jit(solution)/shard_map/tile/pallas_call | solution.py:225
  38.3 2.4 %collective-permute-start.1 = (bf16[3,2,1,32,512]{4,3,1,2,0:T(8,128)(2,1)S(1)}, bf16[3,2,1,32,512]{4,3,1,2,0:T(8,128)(2,1)S(1)}, u32[]{:S(2)}, u32[]{:S(2)}) collective-permute-start(bf16[3,2,1,32,512]{4,3,1,2,0:T(8,128)(2,1)S(1)} %pad_maximum_fusion.1), channel_id=1, source_target_pairs={{0,2},{2,4},{4,6},{6,8},{8,10},{10,12},{12,14},{14,16},{16,18},{18... | collective-permute-start | bytes 589832 | tf_op jit(solution)/shard_map/ppermute | solution.py:268
  40.7 0.0 all-reduce.2.cloned.1.call-update
  40.8 1.3 collective-permute-start
  42.1 44.2 %psum.15 = f32[1024]{0:T(1024)S(1)} all-reduce(f32[1024]{0:T(1024)S(1)} %bitcast.79), channel_id=1, replica_groups=mesh['tx'=16,'ty'=2] {'tx','ty'}, use_global_device_ids=true, to_apply=%region_2.3 | all-reduce | flops 1024 | bytes 8192 | tf_op jit(solution)/shard_map/psum | solution.py:298
  86.2 0.0 collective-permute-done.1
  86.3 0.0 collective-permute-done
  86.3 1.3 collective-permute-start.2
  87.6 0.6 multiply_reduce_fusion.1
  88.3 4.6 %collective-permute-start.3 = (bf16[3,2,1,32,512]{4,3,1,2,0:T(8,128)(2,1)S(1)}, bf16[3,2,1,32,512]{4,3,1,2,0:T(8,128)(2,1)S(1)}, u32[]{:S(2)}, u32[]{:S(2)}) collective-permute-start(bf16[3,2,1,32,512]{4,3,1,2,0:T(8,128)(2,1)S(1)} %pad_maximum_fusion.3), channel_id=1, source_target_pairs={{0,1},{2,3},{4,5},{6,7},{8,9},{10,11},{12,13},{14,15},{16,17},{18,... | collective-permute-start | bytes 589832 | tf_op jit(solution)/shard_map/ppermute | solution.py:268
  92.8 1.2 collective-permute-done.2
  94.1 1.9 collective-permute-done.3
  96.1 0.7 slice_bitcast_fusion
  96.8 0.7 rev.8
  97.5 89.1 %all-reduce.2.cloned.1.call-done = f32[4,512,512]{2,1,0:T(8,128)} async-done(((f32[4,512,512]{2,1,0:T(8,128)}), f32[4,512,512]{2,1,0:T(8,128)}) %all-reduce.2.cloned.1.call-update) | async-done | bytes 4194320 | tf_op jit(solution)/shard_map/psum | solution.py:298
  186.7 3.9 %multiply_reduce_fusion = f32[]{:T(128)} fusion(f32[4,512,512]{2,1,0:T(8,128)} %all-reduce.2.cloned.1.call-done), kind=kLoop, calls=%fused_computation | loop fusion | flops 2097151 | bytes 4194308 | tf_op jit(solution)/shard_map/reduce_sum | solution.py:299
  191.8 0.6 broadcast_multiply_fusion.1
  192.4 4.7 %broadcast_multiply_fusion = f32[4,512,512]{2,1,0:T(8,128)} fusion(f32[4,512,512]{2,1,0:T(8,128)} %all-reduce.2.cloned.1.call-done, f32[]{:T(128)S(6)} %min_shard_map.3), kind=kLoop, calls=%fused_computation.1 | loop fusion | flops 1048576 | bytes 8388612 | tf_op jit(solution)/shard_map/mul | solution.py:305
  (17 shorter events, 0.2 us)
Async XLA Ops:
  7.2 179.5 %all-reduce.2.cloned.1.call-start = ((), (), s32[]{:S(2)}) async-start(), calls=%async_computation | async-start | bytes 8388608 | tf_op jit(solution)/shard_map/psum | solution.py:298
  7.9 1.2 copy-start
  9.1 1.2 copy-start.1
  10.3 1.0 copy-start.2
  11.4 1.0 copy-start.3
  12.4 1.0 copy-start.4
  13.4 0.9 copy-start.5
  14.4 0.9 copy-start.6
  15.3 0.9 copy-start.7
  16.3 0.9 copy-start.8
  17.2 0.8 copy-start.9
  18.0 0.8 copy-start.10
  18.8 0.7 copy-start.11
  19.4 0.7 copy-start.12
  20.1 0.7 copy-start.13
  20.8 0.7 copy-start.14
  38.3 47.9 %collective-permute-start.1 = (bf16[3,2,1,32,512]{4,3,1,2,0:T(8,128)(2,1)S(1)}, bf16[3,2,1,32,512]{4,3,1,2,0:T(8,128)(2,1)S(1)}, u32[]{:S(2)}, u32[]{:S(2)}) collective-permute-start(bf16[3,2,1,32,512]{4,3,1,2,0:T(8,128)(2,1)S(1)} %pad_maximum_fusion.1), channel_id=1, source_target_pairs={{0,2},{2,4},{4,6},{6,8},{8,10},{10,12},{12,14},{14,16},{16,18},{18... | collective-permute-start | bytes 589832 | tf_op jit(solution)/shard_map/ppermute | solution.py:268
  40.8 45.5 %collective-permute-start = (bf16[3,2,1,32,512]{4,3,1,2,0:T(8,128)(2,1)S(1)}, bf16[3,2,1,32,512]{4,3,1,2,0:T(8,128)(2,1)S(1)}, u32[]{:S(2)}, u32[]{:S(2)}) collective-permute-start(bf16[3,2,1,32,512]{4,3,1,2,0:T(8,128)(2,1)S(1)} %pad_maximum_fusion), channel_id=1, source_target_pairs={{2,0},{4,2},{6,4},{8,6},{10,8},{12,10},{14,12},{16,14},{18,16},{20... | collective-permute-start | bytes 589832 | tf_op jit(solution)/shard_map/ppermute | solution.py:268
  86.3 7.7 %collective-permute-start.2 = (bf16[3,2,1,32,512]{4,3,1,2,0:T(8,128)(2,1)S(1)}, bf16[3,2,1,32,512]{4,3,1,2,0:T(8,128)(2,1)S(1)}, u32[]{:S(2)}, u32[]{:S(2)}) collective-permute-start(bf16[3,2,1,32,512]{4,3,1,2,0:T(8,128)(2,1)S(1)} %pad_maximum_fusion.2), channel_id=1, source_target_pairs={{1,0},{3,2},{5,4},{7,6},{9,8},{11,10},{13,12},{15,14},{17,16},{19,... | collective-permute-start | bytes 589832 | tf_op jit(solution)/shard_map/ppermute | solution.py:268
  88.3 7.7 %collective-permute-start.3 = (bf16[3,2,1,32,512]{4,3,1,2,0:T(8,128)(2,1)S(1)}, bf16[3,2,1,32,512]{4,3,1,2,0:T(8,128)(2,1)S(1)}, u32[]{:S(2)}, u32[]{:S(2)}) collective-permute-start(bf16[3,2,1,32,512]{4,3,1,2,0:T(8,128)(2,1)S(1)} %pad_maximum_fusion.3), channel_id=1, source_target_pairs={{0,1},{2,3},{4,5},{6,7},{8,9},{10,11},{12,13},{14,15},{16,17},{18,... | collective-permute-start | bytes 589832 | tf_op jit(solution)/shard_map/ppermute | solution.py:268
Sparse Core Ops, SparseCore 0:
  40.9 145.7 all-reduce.1

commit v2 on v1

v2 whole, which is shorter than its diff:
```python
import functools

import jax
import jax.numpy as jnp
from jax import lax
from jax.experimental import pallas as pl
from jax.experimental.pallas import tpu as pltpu
from jax.sharding import PartitionSpec as P

OFFSETS = ((-1, -1), (-1, 0), (-1, 1), (0, -1), (0, 1), (1, -1), (1, 0), (1, 1))
F32 = jnp.float32
BF16 = jnp.bfloat16
LANES = 128


def mm(a, b):
    return jnp.dot(a, b, preferred_element_type=F32)


def mm_nt(a, b):
    return lax.dot_general(a, b, (((1,), (1,)), ((), ())), preferred_element_type=F32)


def mm_tn(a, b):
    return lax.dot_general(a, b, (((0,), (0,)), ((), ())), preferred_element_type=F32)


def split(value):
    high = value.astype(BF16)
    return high, (value - high.astype(F32)).astype(BF16)


def sigmoid(value):
    return jax.nn.sigmoid(value)


def silu_slope(pre_act):
    gate = sigmoid(pre_act)
    return gate * (1.0 + pre_act * (1.0 - gate))


def count_edges(nbr_ref, mask_ref, count_ref):
    degree, cells = nbr_ref.shape[2:]
    rows = count_ref.shape[0]
    step = 32
    for lane in range(0, cells, 128):
        ids = []
        for k in range(degree):
            here = nbr_ref[0, 0, k : k + 1, lane : lane + 128]
            real = mask_ref[0, 0, k : k + 1, lane : lane + 128]
            ids.append(jnp.broadcast_to(jnp.where(real > 0, here, -1), (8, 128)))

        def body(chunk, carry):
            base = chunk * step
            for part in range(0, step, 8):
                row = lax.broadcasted_iota(jnp.int32, (8, 128), 0) + (base + part)
                total = jnp.zeros((8, 128), F32)
                for k in range(degree):
                    total = total + jnp.where(ids[k] == row, 1.0, 0.0)
                count_ref[pl.ds(pl.multiple_of(base + part, 8), 8), lane : lane + 128] = total
            return carry

        lax.fori_loop(0, rows // step, body, 0)


def one_hot(ids, rows):
    return lax.broadcasted_iota(jnp.int32, (rows, ids.shape[1]), 0) == ids


def flat_rows(send_ref):
    directions, border = send_ref.shape[2:]
    total = directions * border
    ids = send_ref[0, 0]
    spread = (
        lax.broadcasted_iota(jnp.int32, (border, total), 1) % border
        == lax.broadcasted_iota(jnp.int32, (border, total), 0)
    ).astype(BF16)
    high = mm((ids // 256).astype(F32).astype(BF16), spread)
    low = mm((ids % 256).astype(F32).astype(BF16), spread)
    wide = high * 256.0 + low
    mine = lax.broadcasted_iota(
        jnp.int32, (directions, total), 1
    ) // border == lax.broadcasted_iota(jnp.int32, (directions, total), 0)
    return jnp.sum(jnp.where(mine, wide, 0.0), axis=0, keepdims=True).astype(jnp.int32)


def bits_of(size):
    assert size & (size - 1) == 0
    return size.bit_length() - 1


def stream_orders(tx_size, ty_size):
    tx_bits = [("tx", bit) for bit in range(bits_of(tx_size))]
    ty_bits = [("ty", bit) for bit in range(bits_of(ty_size))]
    first, second, rest = tx_bits[:1], tx_bits[1:2], tx_bits[2:]
    return (
        first + ty_bits + second + rest,
        first + second + rest[:1] + ty_bits + rest[1:],
        first + rest[:1] + ty_bits + second + rest[1:],
    )


def stream_ranges(rows, devices):
    unit = 16 * devices
    units = rows // unit
    assert units * unit == rows and units > 0
    used = min(3, units)
    ranges, start = [], 0
    for stream in range(used):
        size = (units // used + (1 if stream < units % used else 0)) * unit
        ranges.append((start, size))
        start += size
    return ranges


class Exchange:
    def __init__(
        self,
        sizes,
        grads_ref,
        sum_ref,
        sent_ref,
        halo_grad_ref,
        fresh_ref,
        returned_ref,
        work_ref,
        landing_ref,
        gate_acc,
        gate_land,
        square_acc,
        square_land,
        send_sems,
        recv_sems,
        small_send,
        small_recv,
        halo_send,
        halo_recv,
    ):
        self.sizes = sizes
        self.me = {"tx": lax.axis_index("tx"), "ty": lax.axis_index("ty")}
        self.grads, self.sum, self.work, self.landing = grads_ref, sum_ref, work_ref, landing_ref
        self.halo = ((sent_ref, fresh_ref, 1), (halo_grad_ref, returned_ref, -1))
        self.small = ((gate_acc, gate_land), (square_acc, square_land))
        self.sems = (send_sems, recv_sems)
        self.small_sems = (small_send, small_recv)
        self.halo_sems = (halo_send, halo_recv)
        self.orders = stream_orders(*sizes)
        self.steps = len(self.orders[0])
        self.landed = 0
        self.streams = []
        self.smalls = []
        self.sending = []
        self.exchanges = []
        self.squares = None

    def bit(self, where):
        axis, bit = where
        return (self.me[axis] // (1 << bit)) % 2

    def partner(self, where):
        axis, bit = where
        return {axis: self.me[axis] + (1 - 2 * self.bit(where)) * (1 << bit)}

    def inside(self, delta_x, delta_y):
        x, y = self.me["tx"] + delta_x, self.me["ty"] + delta_y
        return (x >= 0) & (x < self.sizes[0]) & (y >= 0) & (y < self.sizes[1])

    def offset(self, delta_x, delta_y):
        return {"tx": self.me["tx"] + delta_x, "ty": self.me["ty"] + delta_y}

    def announce(self):
        barrier = pltpu.get_barrier_semaphore()

        def greet(device):
            pl.semaphore_signal(
                barrier, inc=1, device_id=device, device_id_type=pl.DeviceIdType.MESH
            )

        for where in self.orders[0]:
            greet(self.partner(where))
        for offset in OFFSETS:
            pl.when(self.inside(*offset))(lambda offset=offset: greet(self.offset(*offset)))

    def meet(self):
        barrier = pltpu.get_barrier_semaphore()
        peers = self.steps
        for offset in OFFSETS:
            peers = peers + self.inside(*offset).astype(jnp.int32)
        pl.semaphore_wait(barrier, peers)

    def copy(self, source, target, send, recv, device):
        return pltpu.make_async_remote_copy(
            src_ref=source,
            dst_ref=target,
            send_sem=send,
            recv_sem=recv,
            device_id=device,
            device_id_type=pl.DeviceIdType.MESH,
        )

    def begin(self, copy):
        copy.start()
        self.sending.append(copy)
        return copy

    def send_halo(self, kind):
        source, target, sign = self.halo[kind]
        depth, rows, width = source.shape
        border = rows // 8
        for direction, (delta_x, delta_y) in enumerate(OFFSETS):
            part = pl.ds(direction * border, border)
            goes = self.inside(sign * delta_x, sign * delta_y)
            comes = self.inside(-sign * delta_x, -sign * delta_y)
            copy = self.copy(
                source.at[:, part, :],
                target.at[:, part, :],
                self.halo_sems[0].at[kind, direction],
                self.halo_sems[1].at[kind, direction],
                self.offset(sign * delta_x, sign * delta_y),
            )

            @pl.when(goes)
            def _():
                copy.start()

            @pl.when(jnp.logical_not(comes))
            def _():
                target[:, part, :] = jnp.zeros((depth, border, width), BF16)

            self.exchanges.append((copy, goes, comes))

    def open(self, layer, layers):
        rows = self.grads.shape[0] // layers
        for number, (start, size) in enumerate(
            stream_ranges(rows, self.sizes[0] * self.sizes[1])
        ):
            stream = dict(
                slot=len(self.streams),
                order=self.orders[number],
                low=layer * rows + start,
                span=size,
                step=0,
                past=[],
            )
            self.streams.append(stream)
            self.reduce_start(stream)

    def block(self, start, size):
        return pl.ds(pl.multiple_of(start, 16), size)

    def reduce_start(self, stream):
        step, half = stream["step"], stream["span"] // 2
        where = stream["order"][step]
        bit = self.bit(where)
        stream["past"].append((stream["low"], stream["span"]))
        give = stream["low"] + (1 - bit) * half
        stream["target"] = self.landing.at[pl.ds(self.landed, half), :]
        stream["copy"] = self.begin(
            self.copy(
                self.work.at[self.block(give, half), :],
                stream["target"],
                self.sems[0].at[stream["slot"], step],
                self.sems[1].at[stream["slot"], step],
                self.partner(where),
            )
        )
        stream["low"], stream["span"] = stream["low"] + bit * half, half
        self.landed += half

    def gather_start(self, stream):
        step = stream["step"]
        where = stream["order"][2 * self.steps - 1 - step]
        here = self.block(stream["low"], stream["span"])
        stream["copy"] = self.begin(
            self.copy(
                self.sum.at[here, :],
                self.sum.at[here, :],
                self.sems[0].at[stream["slot"], step],
                self.sems[1].at[stream["slot"], step],
                self.partner(where),
            )
        )
        stream["low"], stream["span"] = stream["past"].pop()

    def advance_one(self, stream):
        stream["copy"].wait_recv()
        step = stream["step"]
        stream["step"] = step + 1
        if step < self.steps:
            here = self.block(stream["low"], stream["span"])
            total = self.grads[here, :] + stream["target"][...].astype(F32)
            if step + 1 < self.steps:
                self.grads[here, :] = total
                self.work[here, :] = total.astype(BF16)
                self.reduce_start(stream)
            else:
                self.sum[here, :] = total.astype(BF16)
                squares = jnp.sum((total * total).reshape(-1, 8, LANES), axis=0)
                self.squares = squares if self.squares is None else self.squares + squares
                self.gather_start(stream)
        elif step + 1 < 2 * self.steps:
            self.gather_start(stream)

    def advance(self):
        for stream in self.streams:
            if stream["step"] < 2 * self.steps:
                self.advance_one(stream)

    def small_start(self, small):
        step, kind = small["step"], small["kind"]
        acc, land = self.small[kind]
        small["copy"] = self.begin(
            self.copy(
                acc.at[step],
                land.at[step],
                self.small_sems[0].at[kind, step],
                self.small_sems[1].at[kind, step],
                self.partner(self.orders[0][step]),
            )
        )

    def open_small(self, kind):
        small = dict(kind=kind, step=0)
        self.small_start(small)
        return small

    def advance_small(self, small):
        step = small["step"]
        acc, land = self.small[small["kind"]]
        small["copy"].wait_recv()
        acc[step + 1] = acc[step] + land[step]
        small["step"] = step + 1
        if step + 1 < self.steps:
            self.small_start(small)

    def open_gate(self, gate_grad):
        acc = self.small[0][0]
        for row in range(acc.shape[1]):
            acc[0, row : row + 1, :] = gate_grad[:, row * LANES : (row + 1) * LANES]
        self.smalls.append(self.open_small(0))

    def finish(self):
        steps = self.steps
        while any(stream["step"] < 2 * steps for stream in self.streams) or any(
            small["step"] < steps for small in self.smalls
        ):
            self.advance()
            for small in self.smalls:
                if small["step"] < steps:
                    self.advance_small(small)
            if len(self.smalls) == 1 and all(stream["step"] >= steps for stream in self.streams):
                self.small[1][0][0] = self.squares
                self.smalls.append(self.open_small(1))
        for copy, goes, comes in self.exchanges:
            pl.when(comes)(copy.wait_recv)
            pl.when(goes)(copy.wait_send)
        for copy in self.sending:
            copy.wait_send()
        gate = self.small[0][0][steps]
        square = jnp.sum(self.small[1][0][steps], keepdims=True)
        return gate, square + jnp.sum(gate * gate, keepdims=True)


LOADED = (
    "nbr",
    "mask",
    "expr",
    "halo_expr",
    "cells",
    "halo",
    "self",
    "neigh",
    "stale_halo",
    "send",
    "cot",
    "stale_ret",
)


def step_kernel(sizes, *refs):
    total = len(LOADED)
    live_ref, lig_ref, rec_ref, gate_ref = refs[:4]
    far = refs[4 : 4 + total]
    fresh_ref, returned_ref, sum_ref, gate_out_ref, clip_ref = refs[4 + total : 9 + total]
    near = refs[9 + total : 9 + 2 * total]
    (
        count_ref,
        adj_t_ref,
        adj_low_ref,
        slope_ref,
        prod_ref,
        genes_ref,
        sent_ref,
        halo_grad_ref,
        grads_ref,
        sems,
    ) = refs[9 + 2 * total : 19 + 2 * total]
    link = Exchange(
        sizes,
        grads_ref,
        sum_ref,
        sent_ref,
        halo_grad_ref,
        fresh_ref,
        returned_ref,
        *refs[19 + 2 * total :],
    )
    link.announce()
    copies = {}
    for position, name in enumerate(LOADED):
        copies[name] = pltpu.make_async_copy(far[position], near[position], sems.at[position])
        copies[name].start()
    place = dict(zip(LOADED, near))

    def arrived(name):
        copies[name].wait()
        return place[name]

    layers = place["self"].shape[0]
    cells, width = place["cells"].shape[2:]
    halo = place["halo"].shape[2]
    joined_rows = cells + halo
    genes = place["expr"].shape[3]
    chunk = halo

    nbr_ref, mask_ref = arrived("nbr"), arrived("mask")
    count_edges(nbr_ref, mask_ref, count_ref)

    receptor_hot = one_hot(rec_ref[...], genes)
    ligand_hot = one_hot(lig_ref[...], genes).astype(BF16)
    gate_high, gate_low = split(gate_ref[...])
    zero = jnp.zeros((), BF16)
    mix = mm_nt(jnp.where(receptor_hot, gate_high, zero), ligand_hot)
    mix = mix + mm_nt(jnp.where(receptor_hot, gate_low, zero), ligand_hot)
    mix_high, mix_low = split(mix)
    expr = arrived("expr")[0, 0]
    scaled_high, scaled_low = split(mm(expr, mix_high) + mm(expr, mix_low))
    genes_ref[0:cells, :] = expr
    genes_ref[cells:, :] = arrived("halo_expr")[0, 0]

    def score_chunk(step, carry):
        rows = pl.ds(pl.multiple_of(step * chunk, chunk), chunk)
        here = genes_ref[rows, :]
        score = mm_nt(here, scaled_high) + mm_nt(here, scaled_low)
        gate = sigmoid(score)
        base = 0.25 * count_ref[rows, :] * gate
        high, low = split(base)
        adj_t_ref[rows, :] = high
        adj_low_ref[rows, :] = low
        slope_ref[rows, :] = base * (1.0 - gate)
        return carry

    lax.fori_loop(0, joined_rows // chunk, score_chunk, 0)

    adjacency = adj_t_ref[...].T
    adjacency_low = adj_low_ref[...].T
    state = arrived("cells")[0, 0]
    halo_ref, self_ref, neigh_ref = arrived("halo"), arrived("self"), arrived("neigh")
    stale_halo_ref = arrived("stale_halo")
    states, full_rows, aggregates, pre_acts = [], [], [], []
    for layer in range(layers):
        halo_rows = halo_ref[0, 0] if layer == 0 else stale_halo_ref[0, 0, layer - 1]
        joined = jnp.concatenate([state, halo_rows], 0)
        aggregate = (mm(adjacency, joined) + mm(adjacency_low, joined)).astype(BF16)
        pre_act = mm(state, self_ref[layer]) + mm(aggregate, neigh_ref[layer])
        states.append(state)
        full_rows.append(joined)
        aggregates.append(aggregate)
        pre_acts.append(pre_act)
        if layer + 1 < layers:
            state = (state.astype(F32) + pre_act * sigmoid(pre_act)).astype(BF16)

    send_table = one_hot(flat_rows(arrived("send")), cells).astype(BF16)
    for layer in range(1, layers):
        sent_ref[layer - 1] = mm_tn(send_table, states[layer]).astype(BF16)
    link.meet()
    link.send_halo(0)

    cot_ref, stale_ret_ref = arrived("cot"), arrived("stale_ret")
    live = lax.broadcasted_iota(jnp.int32, (cells, width), 0) < live_ref[0, 0]
    grad_state = jnp.where(live, cot_ref[0, 0].astype(F32), 0.0)
    grad_aggregates = [None] * layers
    for layer in range(layers - 1, -1, -1):
        grad_pre = (grad_state * silu_slope(pre_acts[layer])).astype(BF16)
        for position, left in enumerate((states[layer], aggregates[layer])):
            product = mm_tn(left, grad_pre)
            for lane in range(0, width, LANES):
                start = (2 * layer + position) * width * width // LANES + lane // LANES * width
                grads_ref[start : start + width, :] = product[:, lane : lane + LANES]
                link.work[start : start + width, :] = product[:, lane : lane + LANES].astype(BF16)
        link.open(layer, layers)
        grad_aggregate = mm_nt(grad_pre, neigh_ref[layer]).astype(BF16)
        grad_aggregates[layer] = grad_aggregate
        if layer > 0:
            grad_full = mm(adj_t_ref[...], grad_aggregate)
            halo_grad_ref[layer - 1] = grad_full[cells:].astype(BF16)
            grad_state = (
                grad_state
                + mm_nt(grad_pre, self_ref[layer])
                + grad_full[:cells]
                + mm(send_table, stale_ret_ref[0, 0, layer - 1])
            )
            link.advance()
    link.send_halo(1)

    for start in range(0, joined_rows, chunk):
        inner = jnp.zeros((chunk, cells), F32)
        for layer in range(layers):
            inner = inner + mm_nt(
                full_rows[layer][start : start + chunk], grad_aggregates[layer]
            )
        score_grad = (slope_ref[start : start + chunk, :] * inner).astype(BF16)
        prod_ref[start : start + chunk, :] = mm(score_grad, expr).astype(BF16)
        link.advance()
    pair_grads = mm_tn(genes_ref[...], prod_ref[...]).astype(BF16)
    link.advance()
    picked = mm(pair_grads, receptor_hot.astype(BF16))
    gate_grad = jnp.sum(picked * ligand_hot.astype(F32), axis=0, keepdims=True)
    link.open_gate(gate_grad)
    gate_sum, square = link.finish()
    clip = jnp.minimum(1.0, 2.0 * width / jnp.sqrt(square + 1e-06))
    clip_ref[...] = jnp.broadcast_to(clip, clip_ref.shape)
    gate_out_ref[...] = gate_sum * clip


def run_step(sizes, *args):
    (
        cells,
        halo_inputs,
        stale_halo,
        stale_returned,
        cotangent,
        expression,
        halo_expression,
        neighbours,
        edge_mask,
        send_rows,
        live_cells,
        ligand_genes,
        receptor_genes,
        gate_weights,
        self_weights,
        neighbour_weights,
    ) = args
    layers, width, _ = self_weights.shape
    count, halo = cells.shape[2], halo_inputs.shape[2]
    genes, pairs = expression.shape[3], ligand_genes.shape[0]
    vmem = pl.BlockSpec(memory_space=pltpu.VMEM)
    smem = pl.BlockSpec(memory_space=pltpu.SMEM)
    hbm = pl.BlockSpec(memory_space=pltpu.HBM)
    named = dict(
        nbr=neighbours,
        mask=edge_mask,
        expr=expression,
        halo_expr=halo_expression,
        cells=cells,
        halo=halo_inputs,
        self=self_weights,
        neigh=neighbour_weights,
        stale_halo=stale_halo,
        send=send_rows,
        cot=cotangent,
        stale_ret=stale_returned,
    )
    loaded = [named[name] for name in LOADED]
    rows = 2 * layers * width * width // LANES
    steps = bits_of(sizes[0] * sizes[1])
    streams = layers * len(stream_ranges(rows // layers, sizes[0] * sizes[1]))
    edges = (layers - 1, halo, width)
    gate_tile = (pairs // LANES, LANES)
    return pl.pallas_call(
        functools.partial(step_kernel, sizes),
        out_shape=(
            jax.ShapeDtypeStruct(edges, BF16),
            jax.ShapeDtypeStruct(edges, BF16),
            jax.ShapeDtypeStruct((rows, LANES), BF16),
            jax.ShapeDtypeStruct(gate_tile, F32),
            jax.ShapeDtypeStruct((8, LANES), F32),
        ),
        in_specs=[smem] + [vmem] * 3 + [hbm] * len(loaded),
        out_specs=(vmem,) * 5,
        scratch_shapes=[pltpu.VMEM(value.shape, value.dtype) for value in loaded]
        + [
            pltpu.VMEM((count + halo, count), F32),
            pltpu.VMEM((count + halo, count), BF16),
            pltpu.VMEM((count + halo, count), BF16),
            pltpu.VMEM((count + halo, count), F32),
            pltpu.VMEM((count + halo, genes), BF16),
            pltpu.VMEM((count + halo, genes), BF16),
            pltpu.VMEM(edges, BF16),
            pltpu.VMEM(edges, BF16),
            pltpu.VMEM((rows, LANES), F32),
            pltpu.SemaphoreType.DMA((len(loaded),)),
            pltpu.VMEM((rows, LANES), BF16),
            pltpu.VMEM((rows, LANES), BF16),
            pltpu.VMEM((steps + 1,) + gate_tile, F32),
            pltpu.VMEM((steps + 1,) + gate_tile, F32),
            pltpu.VMEM((steps + 1, 8, LANES), F32),
            pltpu.VMEM((steps + 1, 8, LANES), F32),
            pltpu.SemaphoreType.DMA((streams, 2 * steps)),
            pltpu.SemaphoreType.DMA((streams, 2 * steps)),
            pltpu.SemaphoreType.DMA((2, steps)),
            pltpu.SemaphoreType.DMA((2, steps)),
            pltpu.SemaphoreType.DMA((2, 8)),
            pltpu.SemaphoreType.DMA((2, 8)),
        ],
        compiler_params=pltpu.CompilerParams(
            collective_id=0, has_side_effects=True, vmem_limit_bytes=58 * 1024 * 1024
        ),
        name="step",
    )(
        live_cells,
        ligand_genes.reshape(1, -1),
        receptor_genes.reshape(1, -1),
        gate_weights.reshape(1, -1),
        *loaded,
    )


def on_device(sizes, *args):
    self_weights = args[14]
    layers, width, _ = self_weights.shape
    fresh, returned, layer_sum, gate, clip = run_step(sizes, *args)
    halo_shape = (1, 1) + fresh.shape
    blocks = layer_sum.reshape(2 * layers, width // LANES, width, LANES)
    blocks = blocks.transpose(0, 2, 1, 3).reshape(2 * layers, width, width)
    return (
        fresh.reshape(halo_shape),
        returned.reshape(halo_shape),
        clip[0, 0] * blocks.astype(F32),
        gate.reshape(-1),
    )


def solution(mesh):
    tile = P("tx", "ty")
    sizes = (mesh.shape["tx"], mesh.shape["ty"])
    return jax.shard_map(
        functools.partial(on_device, sizes),
        mesh=mesh,
        in_specs=(tile,) * 11 + (P(),) * 5,
        out_specs=(tile, tile, P(), P()),
        check_vma=False,
    )
```

time: 205 us -> 68 us (0.33)
  waiting for transfers between devices: 92.3 us -> 0 us
  blocking collectives: 44.2 us -> 0 us
  Pallas kernels: 16.7 us -> 58.1 us
  between operations: 16.1 us -> 1.32 us
  starting transfers between devices: 9.58 us -> 0 us
  local copies, waits for them, and re-layouts: 15.2 us -> 5.82 us
  other arithmetic: 9.91 us -> 2.51 us
    psum x1 -> x0, waiting for transfers between devices: 89.1 us -> none  [on_device(): layer_sum, gate_sum = lax.psum((layer_grads, gate_grad[0]), ('tx', 'ty'))]
    psum x1 -> x0, blocking collectives: 44.2 us -> none  [on_device(): layer_sum, gate_sum = lax.psum((layer_grads, gate_grad[0]), ('tx', 'ty'))]
    pallas_call x1, Pallas kernels: 16.7 us -> 58.1 us  [run_step(): pl.pallas_call(functools.partial(step_kernel, sizes), out_shape=(jax.Shap...]
    unnamed x37 -> x9, local copies, waits for them, and re-layouts: 13.7 us -> 2.01 us
    ppermute x4 -> x0, starting transfers between devices: 9.54 us -> none  [shift(): lax.ppermute(value, axis, [(source, source + steps) for source in range(f...]
    reduce_sum x2 -> x0, other arithmetic: 4.47 us -> none  [on_device(): square = jnp.sum(layer_sum * layer_sum) + jnp.sum(gate_sum * gate_sum)]
    ppermute x4 -> x0, waiting for transfers between devices: 3.15 us -> none  [shift(): lax.ppermute(value, axis, [(source, source + steps) for source in range(f...]
    mul x2 -> x1, other arithmetic: 5.29 us -> 2.51 us  [on_device(): clip[0, 0] * blocks.astype(F32)]
  transfers between devices with their start and end apart: 5 -> 0, of which waited for: 3 -> 0; matrix products, arithmetic and copies ran while one was open for 1% -> 0% of each run, Pallas kernels for 0% -> 0%
where the time goes in v2:
time: 68 us; the launch traced here: 67.8 us
  Pallas kernels  58.1 us (85%)
  local copies, waits for them, and re-layouts  5.82 us (9%)
  other arithmetic  2.51 us (4%)
  between operations  1.32 us (2%)
    pallas_call x1, Pallas kernels, run_step(): pl.pallas_call(functools.partial(step_kernel, sizes), out_shape=(jax.Shap...  58.1 us
    mul x1, local copies, waits for them, and re-layouts, on_device(): clip[0, 0] * blocks.astype(F32)  2.61 us
    mul x1, other arithmetic, on_device(): clip[0, 0] * blocks.astype(F32)  2.51 us
    unnamed x9, local copies, waits for them, and re-layouts  2.01 us

profile of v2, /device:TPU:0, one launch (start us, length us, event | category | flops | bytes accessed | tf_op | source)
XLA Modules:
  0.0 67.8 jit_solution(2332834750900455621)
XLA Ops:
  1.3 58.1 %step.1 = (bf16[1,256,512]{2,1,0:T(8,128)(2,1)}, bf16[1,256,512]{2,1,0:T(8,128)(2,1)}, bf16[8192,128]{1,0:T(8,128)(2,1)}, f32[8,128]{1,0:T(8,128)}, f32[8,128]{1,0:T(8,128)}) custom-call(s32[1,1]{1,0:T(1,128)S(6)} %copy.27.refs_0_, s32[1,1024]{1,0:T(1,128)} %bitcast.18, s32[1,1024]{1,0:T(1,128)} %bitcast.19, f32[1,1024]{1,0:T(1,128)} %bitcast.20, ...), custom_call_target="tpu_custom_call" | custom-call | tf_op jit(solution)/shard_map/step/pallas_call | solution.py:571
  59.4 1.2 %slice.3 = f32[1,1]{1,0:T(1,128)} slice(f32[8,128]{1,0:T(8,128)} %get-tuple-element.11), slice={[0:1], [0:1]} | slice | bytes 8 | tf_op jit(solution)/shard_map/slice | solution.py:630
  60.6 2.5 %convert_multiply_fusion = f32[8192,128]{1,0:T(8,128)S(1)} fusion(bf16[8192,128]{1,0:T(8,128)(2,1)} %get-tuple-element.12, f32[]{:T(128)} %bitcast.5), kind=kLoop, calls=%fused_computation.1 | loop fusion | flops 2097152 | bytes 6291460 | tf_op jit(solution)/shard_map/mul | solution.py:630
  63.1 0.0 copy-start.1
  63.1 0.0 copy-start
  63.1 0.0 copy-start.2
  63.1 2.6 %copy.23 = f32[4,4,64,8,128]{4,3,1,2,0:T(8,128)} copy(f32[4,4,64,8,128]{4,3,2,1,0:T(8,128)S(1)} %bitcast.14) | data formatting | bytes 8388608 | tf_op jit(solution)/shard_map/mul | solution.py:630
  65.8 0.0 copy-done.1
  65.8 0.7 %copy.28 = bf16[1,1,1,256,512]{4,3,2,1,0:T(8,128)(2,1)} copy(bf16[1,1,1,256,512]{4,3,2,1,0:T(8,128)(2,1)S(1)} %bitcast.17) | data formatting | bytes 524288
  66.5 0.0 copy-done
  66.5 0.7 %copy.29 = bf16[1,1,1,256,512]{4,3,2,1,0:T(8,128)(2,1)} copy(bf16[1,1,1,256,512]{4,3,2,1,0:T(8,128)(2,1)S(1)} %bitcast.16) | data formatting | bytes 524288
  67.2 0.0 copy-done.2
  67.2 0.6 copy.30
Async XLA Ops:
  63.1 2.6 %copy-start.1 = (bf16[1,256,512]{2,1,0:T(8,128)(2,1)S(1)}, bf16[1,256,512]{2,1,0:T(8,128)(2,1)}, u32[]{:S(2)}) copy-start(bf16[1,256,512]{2,1,0:T(8,128)(2,1)} %get-tuple-element.9) | copy-start | bytes 786436
  63.1 3.3 %copy-start = (bf16[1,256,512]{2,1,0:T(8,128)(2,1)S(1)}, bf16[1,256,512]{2,1,0:T(8,128)(2,1)}, u32[]{:S(2)}) copy-start(bf16[1,256,512]{2,1,0:T(8,128)(2,1)} %get-tuple-element.10) | copy-start | bytes 786436
  63.1 4.0 %copy-start.2 = (f32[8,128]{1,0:T(8,128)S(1)}, f32[8,128]{1,0:T(8,128)}, u32[]{:S(2)}) copy-start(f32[8,128]{1,0:T(8,128)} %get-tuple-element.13) | copy-start | bytes 12292

commit v3 on v2

--- a/solution.py
+++ b/solution.py
@@ -42,25 +42,30 @@
 def count_edges(nbr_ref, mask_ref, count_ref):
     degree, cells = nbr_ref.shape[2:]
     rows = count_ref.shape[0]
-    step = 32
+    step, group = 64, 256
     for lane in range(0, cells, 128):
-        ids = []
-        for k in range(degree):
-            here = nbr_ref[0, 0, k : k + 1, lane : lane + 128]
-            real = mask_ref[0, 0, k : k + 1, lane : lane + 128]
-            ids.append(jnp.broadcast_to(jnp.where(real > 0, here, -1), (8, 128)))
-
-        def body(chunk, carry):
-            base = chunk * step
-            for part in range(0, step, 8):
-                row = lax.broadcasted_iota(jnp.int32, (8, 128), 0) + (base + part)
-                total = jnp.zeros((8, 128), F32)
-                for k in range(degree):
-                    total = total + jnp.where(ids[k] == row, 1.0, 0.0)
-                count_ref[pl.ds(pl.multiple_of(base + part, 8), 8), lane : lane + 128] = total
-            return carry
-
-        lax.fori_loop(0, rows // step, body, 0)
+        for first in range(0, rows, group):
+            ids = []
+            for k in range(degree):
+                here = nbr_ref[0, 0, k : k + 1, lane : lane + 128] - first
+                real = mask_ref[0, 0, k : k + 1, lane : lane + 128]
+                near = jnp.where(real > 0, here, -1).astype(F32)
+                ids.append(jnp.broadcast_to(near, (16, 128)).astype(BF16))
+
+            def body(chunk, carry):
+                for part in range(0, step, 16):
+                    base = chunk * step + part
+                    row = lax.broadcasted_iota(jnp.int32, (16, 128), 0) + base
+                    row = row.astype(F32).astype(BF16)
+                    total = jnp.zeros((16, 128), BF16)
+                    one = jnp.ones((16, 128), BF16)
+                    for k in range(degree):
+                        total = total + jnp.where(ids[k] == row, one, jnp.zeros_like(one))
+                    start = pl.multiple_of(first + base, 16)
+                    count_ref[pl.ds(start, 16), lane : lane + 128] = total
+                return carry
+
+            lax.fori_loop(0, min(group, rows - first) // step, body, 0)
 
 
 def one_hot(ids, rows):
@@ -443,7 +448,7 @@
         here = genes_ref[rows, :]
         score = mm_nt(here, scaled_high) + mm_nt(here, scaled_low)
         gate = sigmoid(score)
-        base = 0.25 * count_ref[rows, :] * gate
+        base = 0.25 * count_ref[rows, :].astype(F32) * gate
         high, low = split(base)
         adj_t_ref[rows, :] = high
         adj_low_ref[rows, :] = low
@@ -520,7 +525,7 @@
     gate_sum, square = link.finish()
     clip = jnp.minimum(1.0, 2.0 * width / jnp.sqrt(square + 1e-06))
     clip_ref[...] = jnp.broadcast_to(clip, clip_ref.shape)
-    gate_out_ref[...] = gate_sum * clip
+    gate_out_ref[...] = gate_sum
 
 
 def run_step(sizes, *args):
@@ -581,7 +586,7 @@
         out_specs=(vmem,) * 5,
         scratch_shapes=[pltpu.VMEM(value.shape, value.dtype) for value in loaded]
         + [
-            pltpu.VMEM((count + halo, count), F32),
+            pltpu.VMEM((count + halo, count), BF16),
             pltpu.VMEM((count + halo, count), BF16),
             pltpu.VMEM((count + halo, count), BF16),
             pltpu.VMEM((count + halo, count), F32),
@@ -617,19 +622,92 @@
     )
 
 
+def finish_kernel(
+    fresh_ref,
+    returned_ref,
+    sum_ref,
+    clip_ref,
+    gate_ref,
+    fresh_out,
+    returned_out,
+    layer_out,
+    gate_out,
+    sum_near,
+    layer_near,
+    pass_sems,
+    load_sems,
+    store_sems,
+):
+    count, width, _ = layer_near.shape
+    span = width * width // LANES
+    passes = []
+    for position, (source, target) in enumerate(
+        ((fresh_ref, fresh_out), (returned_ref, returned_out))
+    ):
+        passes.append(
+            pltpu.make_async_copy(source, target.at[0, 0], pass_sems.at[position])
+        )
+    loads = [
+        pltpu.make_async_copy(
+            sum_ref.at[pl.ds(index * span, span), :],
+            sum_near.at[pl.ds(index * span, span), :],
+            load_sems.at[index],
+        )
+        for index in range(count)
+    ]
+    stores = [
+        pltpu.make_async_copy(layer_near.at[index], layer_out.at[index], store_sems.at[index])
+        for index in range(count)
+    ]
+    for copy in loads + passes:
+        copy.start()
+    clip = clip_ref[0:1, 0:1]
+    gate_out[...] = gate_ref[...] * clip
+    for index in range(count):
+        loads[index].wait()
+        for lane in range(0, width, LANES):
+            start = index * span + lane // LANES * width
+            part = sum_near[start : start + width, :].astype(F32)
+            layer_near[index, :, lane : lane + LANES] = part * clip
+        stores[index].start()
+    for copy in stores + passes:
+        copy.wait()
+
+
+def finish(layers, width, fresh, returned, layer_sum, clip, gate):
+    hbm = pl.BlockSpec(memory_space=pltpu.HBM)
+    vmem = pl.BlockSpec(memory_space=pltpu.VMEM)
+    count = 2 * layers
+    return pl.pallas_call(
+        finish_kernel,
+        out_shape=(
+            jax.ShapeDtypeStruct((1, 1) + fresh.shape, BF16),
+            jax.ShapeDtypeStruct((1, 1) + fresh.shape, BF16),
+            jax.ShapeDtypeStruct((count, width, width), F32),
+            jax.ShapeDtypeStruct(gate.shape, F32),
+        ),
+        in_specs=[hbm, hbm, hbm, vmem, vmem],
+        out_specs=(hbm, hbm, hbm, vmem),
+        scratch_shapes=[
+            pltpu.VMEM(layer_sum.shape, BF16),
+            pltpu.VMEM((count, width, width), F32),
+            pltpu.SemaphoreType.DMA((2,)),
+            pltpu.SemaphoreType.DMA((count,)),
+            pltpu.SemaphoreType.DMA((count,)),
+        ],
+        compiler_params=pltpu.CompilerParams(vmem_limit_bytes=58 * 1024 * 1024),
+        name="finish",
+    )(fresh, returned, layer_sum, clip, gate)
+
+
 def on_device(sizes, *args):
     self_weights = args[14]
     layers, width, _ = self_weights.shape
     fresh, returned, layer_sum, gate, clip = run_step(sizes, *args)
-    halo_shape = (1, 1) + fresh.shape
-    blocks = layer_sum.reshape(2 * layers, width // LANES, width, LANES)
-    blocks = blocks.transpose(0, 2, 1, 3).reshape(2 * layers, width, width)
-    return (
-        fresh.reshape(halo_shape),
-        returned.reshape(halo_shape),
-        clip[0, 0] * blocks.astype(F32),
-        gate.reshape(-1),
+    fresh, returned, layer_part, gate = finish(
+        layers, width, fresh, returned, layer_sum, clip, gate
     )
+    return fresh, returned, layer_part, gate.reshape(-1)
 
 
 def solution(mesh):

time: 68 us -> 76.7 us (1.13)
  Pallas kernels: 58.1 us -> 75 us
  local copies, waits for them, and re-layouts: 5.82 us -> 0 us
  other arithmetic: 2.51 us -> 0 us
    pallas_call x0 -> x1, Pallas kernels: none -> 18.4 us  [finish(): pl.pallas_call(finish_kernel, out_shape=(jax.ShapeDtypeStruct((1, 1) + fr...]
    mul x1 -> x0, local copies, waits for them, and re-layouts: 2.61 us -> none  [on_device(): clip[0, 0] * blocks.astype(F32)]
    mul x1 -> x0, other arithmetic: 2.51 us -> none  [on_device(): clip[0, 0] * blocks.astype(F32)]
    unnamed x9 -> x0, local copies, waits for them, and re-layouts: 2.01 us -> none
    pallas_call x1, Pallas kernels: 58.1 us -> 56.6 us  [run_step(): pl.pallas_call(functools.partial(step_kernel, sizes), out_shape=(jax.Shap...]
    slice x1 -> x0, local copies, waits for them, and re-layouts: 1.2 us -> none  [on_device(): clip[0, 0] * blocks.astype(F32)]
where the time goes in v3:
time: 76.7 us; the launch traced here: 76.5 us
  Pallas kernels  75 us (98%)
  between operations  1.45 us (2%)
    pallas_call x1, Pallas kernels, run_step(): pl.pallas_call(functools.partial(step_kernel, sizes), out_shape=(jax.Shap...  56.6 us
    pallas_call x1, Pallas kernels, finish(): pl.pallas_call(finish_kernel, out_shape=(jax.ShapeDtypeStruct((1, 1) + fr...  18.4 us

profile of v3, /device:TPU:0, one launch (start us, length us, event | category | flops | bytes accessed | tf_op | source)
XLA Modules:
  0.0 76.5 jit_solution(6079534040318253187)
XLA Ops:
  1.3 56.6 %step.1 = (bf16[1,256,512]{2,1,0:T(8,128)(2,1)}, bf16[1,256,512]{2,1,0:T(8,128)(2,1)}, bf16[8192,128]{1,0:T(8,128)(2,1)}, f32[8,128]{1,0:T(8,128)}, f32[8,128]{1,0:T(8,128)}) custom-call(s32[1,1]{1,0:T(1,128)S(6)} %copy.20.refs_0_, s32[1,1024]{1,0:T(1,128)} %bitcast.4, s32[1,1024]{1,0:T(1,128)} %bitcast.5, f32[1,1024]{1,0:T(1,128)} %bitcast.6, ...), custom_call_target="tpu_custom_call" | custom-call | tf_op jit(solution)/shard_map/step/pallas_call | solution.py:576
  57.9 18.4 %finish.1 = (bf16[1,1,1,256,512]{4,3,2,1,0:T(8,128)(2,1)}, bf16[1,1,1,256,512]{4,3,2,1,0:T(8,128)(2,1)}, f32[4,512,512]{2,1,0:T(8,128)}, f32[8,128]{1,0:T(8,128)}) custom-call(bf16[1,256,512]{2,1,0:T(8,128)(2,1)} %get-tuple-element.13.fresh_ref, bf16[1,256,512]{2,1,0:T(8,128)(2,1)} %get-tuple-element.14.returned_ref, ...), custom_call_target="tpu_custom_call" | custom-call | tf_op jit(solution)/shard_map/finish/pallas_call | solution.py:681

commit v4 on v3

--- a/solution.py
+++ b/solution.py
@@ -97,12 +97,16 @@
 def stream_orders(tx_size, ty_size):
     tx_bits = [("tx", bit) for bit in range(bits_of(tx_size))]
     ty_bits = [("ty", bit) for bit in range(bits_of(ty_size))]
-    first, second, rest = tx_bits[:1], tx_bits[1:2], tx_bits[2:]
-    return (
-        first + ty_bits + second + rest,
-        first + second + rest[:1] + ty_bits + rest[1:],
-        first + rest[:1] + ty_bits + second + rest[1:],
-    )
+
+    def paired(bits):
+        return [tuple(bits[at : at + 2]) for at in range(0, len(bits), 2)]
+
+    first, near, far = paired(tx_bits[:1]), paired(ty_bits + tx_bits[1:2]), paired(tx_bits[2:])
+    return (first + near + far, first + near + far, first + far + near)
+
+
+def messages_of(order):
+    return sum((1 << len(stage)) - 1 for stage in order)
 
 
 def stream_ranges(rows, devices):
@@ -162,9 +166,19 @@
         axis, bit = where
         return (self.me[axis] // (1 << bit)) % 2
 
-    def partner(self, where):
-        axis, bit = where
-        return {axis: self.me[axis] + (1 - 2 * self.bit(where)) * (1 << bit)}
+    def partner(self, stage, flips):
+        place = dict(self.me)
+        for position, where in enumerate(stage):
+            if flips >> position & 1:
+                place[where[0]] = place[where[0]] + (1 - 2 * self.bit(where)) * (1 << where[1])
+        return place
+
+    def digit(self, stage, flips):
+        total = 0
+        for position, where in enumerate(stage):
+            bit = self.bit(where)
+            total = total + ((1 - bit) if flips >> position & 1 else bit) * (1 << position)
+        return total
 
     def inside(self, delta_x, delta_y):
         x, y = self.me["tx"] + delta_x, self.me["ty"] + delta_y
@@ -181,14 +195,15 @@
                 barrier, inc=1, device_id=device, device_id_type=pl.DeviceIdType.MESH
             )
 
-        for where in self.orders[0]:
-            greet(self.partner(where))
+        for stage in self.orders[0]:
+            for flips in range(1, 1 << len(stage)):
+                greet(self.partner(stage, flips))
         for offset in OFFSETS:
             pl.when(self.inside(*offset))(lambda offset=offset: greet(self.offset(*offset)))
 
     def meet(self):
         barrier = pltpu.get_barrier_semaphore()
-        peers = self.steps
+        peers = messages_of(self.orders[0])
         for offset in OFFSETS:
             peers = peers + self.inside(*offset).astype(jnp.int32)
         pl.semaphore_wait(barrier, peers)
@@ -241,10 +256,12 @@
         ):
             stream = dict(
                 slot=len(self.streams),
+                layer=layer,
                 order=self.orders[number],
                 low=layer * rows + start,
                 span=size,
                 step=0,
+                sent=0,
                 past=[],
             )
             self.streams.append(stream)
@@ -253,47 +270,54 @@
     def block(self, start, size):
         return pl.ds(pl.multiple_of(start, 16), size)
 
-    def reduce_start(self, stream):
-        step, half = stream["step"], stream["span"] // 2
-        where = stream["order"][step]
-        bit = self.bit(where)
-        stream["past"].append((stream["low"], stream["span"]))
-        give = stream["low"] + (1 - bit) * half
-        stream["target"] = self.landing.at[pl.ds(self.landed, half), :]
-        stream["copy"] = self.begin(
+    def send_part(self, stream, source, target, stage, flips):
+        number = stream["sent"]
+        stream["sent"] = number + 1
+        return self.begin(
             self.copy(
-                self.work.at[self.block(give, half), :],
-                stream["target"],
-                self.sems[0].at[stream["slot"], step],
-                self.sems[1].at[stream["slot"], step],
-                self.partner(where),
+                source,
+                target,
+                self.sems[0].at[stream["slot"], number],
+                self.sems[1].at[stream["slot"], number],
+                self.partner(stage, flips),
             )
         )
-        stream["low"], stream["span"] = stream["low"] + bit * half, half
-        self.landed += half
+
+    def reduce_start(self, stream):
+        stage = stream["order"][stream["step"]]
+        radix = 1 << len(stage)
+        piece = stream["span"] // radix
+        stream["past"].append((stream["low"], stream["span"]))
+        stream["copies"], stream["targets"] = [], []
+        for flips in range(1, radix):
+            give = stream["low"] + self.digit(stage, flips) * piece
+            target = self.landing.at[pl.ds(self.landed, piece), :]
+            source = self.work.at[self.block(give, piece), :]
+            stream["copies"].append(self.send_part(stream, source, target, stage, flips))
+            stream["targets"].append(target)
+            self.landed += piece
+        stream["low"] = stream["low"] + self.digit(stage, 0) * piece
+        stream["span"] = piece
 
     def gather_start(self, stream):
-        step = stream["step"]
-        where = stream["order"][2 * self.steps - 1 - step]
-        here = self.block(stream["low"], stream["span"])
-        stream["copy"] = self.begin(
-            self.copy(
-                self.sum.at[here, :],
-                self.sum.at[here, :],
-                self.sems[0].at[stream["slot"], step],
-                self.sems[1].at[stream["slot"], step],
-                self.partner(where),
-            )
-        )
+        stage = stream["order"][2 * self.steps - 1 - stream["step"]]
+        here = self.sum.at[self.block(stream["low"], stream["span"]), :]
+        stream["copies"] = [
+            self.send_part(stream, here, here, stage, flips)
+            for flips in range(1, 1 << len(stage))
+        ]
         stream["low"], stream["span"] = stream["past"].pop()
 
     def advance_one(self, stream):
-        stream["copy"].wait_recv()
+        for copy in stream["copies"]:
+            copy.wait_recv()
         step = stream["step"]
         stream["step"] = step + 1
         if step < self.steps:
             here = self.block(stream["low"], stream["span"])
-            total = self.grads[here, :] + stream["target"][...].astype(F32)
+            total = self.grads[here, :]
+            for target in stream["targets"]:
+                total = total + target[...].astype(F32)
             if step + 1 < self.steps:
                 self.grads[here, :] = total
                 self.work[here, :] = total.astype(BF16)
@@ -306,23 +330,28 @@
         elif step + 1 < 2 * self.steps:
             self.gather_start(stream)
 
-    def advance(self):
+    def advance(self, layer=None):
         for stream in self.streams:
-            if stream["step"] < 2 * self.steps:
+            if stream["step"] < 2 * self.steps and layer in (None, stream["layer"]):
                 self.advance_one(stream)
 
     def small_start(self, small):
         step, kind = small["step"], small["kind"]
         acc, land = self.small[kind]
-        small["copy"] = self.begin(
-            self.copy(
+        stage = self.orders[0][step]
+        first = messages_of(self.orders[0][:step])
+        small["slots"], small["copies"] = [], []
+        for flips in range(1, 1 << len(stage)):
+            slot = first + flips - 1
+            copy = self.copy(
                 acc.at[step],
-                land.at[step],
-                self.small_sems[0].at[kind, step],
-                self.small_sems[1].at[kind, step],
-                self.partner(self.orders[0][step]),
+                land.at[slot],
+                self.small_sems[0].at[kind, slot],
+                self.small_sems[1].at[kind, slot],
+                self.partner(stage, flips),
             )
-        )
+            small["copies"].append(self.begin(copy))
+            small["slots"].append(slot)
 
     def open_small(self, kind):
         small = dict(kind=kind, step=0)
@@ -332,8 +361,12 @@
     def advance_small(self, small):
         step = small["step"]
         acc, land = self.small[small["kind"]]
-        small["copy"].wait_recv()
-        acc[step + 1] = acc[step] + land[step]
+        for copy in small["copies"]:
+            copy.wait_recv()
+        terms = [acc[step]] + [land[slot] for slot in small["slots"]]
+        while len(terms) > 1:
+            terms = [terms[at] + terms[at + 1] for at in range(0, len(terms), 2)]
+        acc[step + 1] = terms[0]
         small["step"] = step + 1
         if step + 1 < self.steps:
             self.small_start(small)
@@ -505,7 +538,7 @@
                 + grad_full[:cells]
                 + mm(send_table, stale_ret_ref[0, 0, layer - 1])
             )
-            link.advance()
+            link.advance(layer)
     link.send_halo(1)
 
     for start in range(0, joined_rows, chunk):
@@ -516,9 +549,9 @@
             )
         score_grad = (slope_ref[start : start + chunk, :] * inner).astype(BF16)
         prod_ref[start : start + chunk, :] = mm(score_grad, expr).astype(BF16)
-        link.advance()
+        if start < layers * chunk:
+            link.advance(start // chunk)
     pair_grads = mm_tn(genes_ref[...], prod_ref[...]).astype(BF16)
-    link.advance()
     picked = mm(pair_grads, receptor_hot.astype(BF16))
     gate_grad = jnp.sum(picked * ligand_hot.astype(F32), axis=0, keepdims=True)
     link.open_gate(gate_grad)
@@ -569,7 +602,8 @@
     )
     loaded = [named[name] for name in LOADED]
     rows = 2 * layers * width * width // LANES
-    steps = bits_of(sizes[0] * sizes[1])
+    order = stream_orders(*sizes)[0]
+    steps, messages = len(order), messages_of(order)
     streams = layers * len(stream_ranges(rows // layers, sizes[0] * sizes[1]))
     edges = (layers - 1, halo, width)
     gate_tile = (pairs // LANES, LANES)
@@ -599,13 +633,13 @@
             pltpu.VMEM((rows, LANES), BF16),
             pltpu.VMEM((rows, LANES), BF16),
             pltpu.VMEM((steps + 1,) + gate_tile, F32),
-            pltpu.VMEM((steps + 1,) + gate_tile, F32),
+            pltpu.VMEM((messages,) + gate_tile, F32),
             pltpu.VMEM((steps + 1, 8, LANES), F32),
-            pltpu.VMEM((steps + 1, 8, LANES), F32),
-            pltpu.SemaphoreType.DMA((streams, 2 * steps)),
-            pltpu.SemaphoreType.DMA((streams, 2 * steps)),
-            pltpu.SemaphoreType.DMA((2, steps)),
-            pltpu.SemaphoreType.DMA((2, steps)),
+            pltpu.VMEM((messages, 8, LANES), F32),
+            pltpu.SemaphoreType.DMA((streams, 2 * messages)),
+            pltpu.SemaphoreType.DMA((streams, 2 * messages)),
+            pltpu.SemaphoreType.DMA((2, messages)),
+            pltpu.SemaphoreType.DMA((2, messages)),
             pltpu.SemaphoreType.DMA((2, 8)),
             pltpu.SemaphoreType.DMA((2, 8)),
         ],
@@ -634,19 +668,22 @@
     gate_out,
     sum_near,
     layer_near,
+    halo_near,
     pass_sems,
     load_sems,
     store_sems,
 ):
     count, width, _ = layer_near.shape
     span = width * width // LANES
-    passes = []
-    for position, (source, target) in enumerate(
-        ((fresh_ref, fresh_out), (returned_ref, returned_out))
-    ):
-        passes.append(
-            pltpu.make_async_copy(source, target.at[0, 0], pass_sems.at[position])
-        )
+    halos = ((fresh_ref, fresh_out), (returned_ref, returned_out))
+    into = [
+        pltpu.make_async_copy(source, halo_near.at[position], pass_sems.at[0, position])
+        for position, (source, _) in enumerate(halos)
+    ]
+    onward = [
+        pltpu.make_async_copy(halo_near.at[position], target.at[0, 0], pass_sems.at[1, position])
+        for position, (_, target) in enumerate(halos)
+    ]
     loads = [
         pltpu.make_async_copy(
             sum_ref.at[pl.ds(index * span, span), :],
@@ -659,7 +696,7 @@
         pltpu.make_async_copy(layer_near.at[index], layer_out.at[index], store_sems.at[index])
         for index in range(count)
     ]
-    for copy in loads + passes:
+    for copy in loads + into:
         copy.start()
     clip = clip_ref[0:1, 0:1]
     gate_out[...] = gate_ref[...] * clip
@@ -670,7 +707,10 @@
             part = sum_near[start : start + width, :].astype(F32)
             layer_near[index, :, lane : lane + LANES] = part * clip
         stores[index].start()
-    for copy in stores + passes:
+    for position in range(len(halos)):
+        into[position].wait()
+        onward[position].start()
+    for copy in stores + onward:
         copy.wait()
 
 
@@ -691,7 +731,8 @@
         scratch_shapes=[
             pltpu.VMEM(layer_sum.shape, BF16),
             pltpu.VMEM((count, width, width), F32),
-            pltpu.SemaphoreType.DMA((2,)),
+            pltpu.VMEM((2,) + fresh.shape, BF16),
+            pltpu.SemaphoreType.DMA((2, 2)),
             pltpu.SemaphoreType.DMA((count,)),
             pltpu.SemaphoreType.DMA((count,)),
         ],

time: 76.7 us -> 58.4 us (0.76)
  Pallas kernels: 75 us -> 56.7 us
    pallas_call x1, Pallas kernels: 18.4 us -> 4.72 us  [finish(): pl.pallas_call(finish_kernel, out_shape=(jax.ShapeDtypeStruct((1, 1) + fr...]
    pallas_call x1, Pallas kernels: 56.6 us -> 52 us  [run_step(): pl.pallas_call(functools.partial(step_kernel, sizes), out_shape=(jax.Shap...]
where the time goes in v4:
time: 58.4 us; the launch traced here: 58.1 us
  Pallas kernels  56.7 us (97%)
  between operations  1.45 us (2%)
    pallas_call x1, Pallas kernels, run_step(): pl.pallas_call(functools.partial(step_kernel, sizes), out_shape=(jax.Shap...  52 us
    pallas_call x1, Pallas kernels, finish(): pl.pallas_call(finish_kernel, out_shape=(jax.ShapeDtypeStruct((1, 1) + fr...  4.72 us

profile of v4, /device:TPU:0, one launch (start us, length us, event | category | flops | bytes accessed | tf_op | source)
XLA Modules:
  0.0 58.1 jit_solution(6593809551501308502)
XLA Ops:
  1.3 52.0 %step.1 = (bf16[1,256,512]{2,1,0:T(8,128)(2,1)}, bf16[1,256,512]{2,1,0:T(8,128)(2,1)}, bf16[8192,128]{1,0:T(8,128)(2,1)}, f32[8,128]{1,0:T(8,128)}, f32[8,128]{1,0:T(8,128)}) custom-call(s32[1,1]{1,0:T(1,128)S(6)} %copy.20.refs_0_, s32[1,1024]{1,0:T(1,128)} %bitcast.4, s32[1,1024]{1,0:T(1,128)} %bitcast.5, f32[1,1024]{1,0:T(1,128)} %bitcast.6, ...), custom_call_target="tpu_custom_call" | custom-call | tf_op jit(solution)/shard_map/step/pallas_call | solution.py:610
  53.3 4.7 %finish.1 = (bf16[1,1,1,256,512]{4,3,2,1,0:T(8,128)(2,1)}, bf16[1,1,1,256,512]{4,3,2,1,0:T(8,128)(2,1)}, f32[4,512,512]{2,1,0:T(8,128)}, f32[8,128]{1,0:T(8,128)}) custom-call(bf16[1,256,512]{2,1,0:T(8,128)(2,1)} %get-tuple-element.13.fresh_ref, bf16[1,256,512]{2,1,0:T(8,128)(2,1)} %get-tuple-element.14.returned_ref, ...), custom_call_target="tpu_custom_call" | custom-call | tf_op jit(solution)/shard_map/finish/pallas_call | solution.py:721
